TPU v7x, 32 devices: a whole 2x2x4 slice. The times are simulated.
32 devices in a mesh: rows: 8 (over z, core), blk: 4 (over y, x).
Axes of the slice: x: 2, y: 2, z: 4, core: 2. Of those that a mesh axis runs over, the one named last changes fastest.
Arguments:
- jacobian: float32 [32768, 1024], P('rows', 'blk'), may hold values from -6 to 6
- row_weight: float32 [32768], P('rows'), may hold values from 0.3 to 3
- col_scale: float32 [1024], P('blk'), may hold values from 0.3 to 3
- round_count: int32 [2], replicated, may hold values from 12 to 24, as said below
- move_flag: int32 [2, 4], P(None, 'blk'), may hold values 0 or 1
Outputs:
- rotated: float32 [32768, 1024], P('rows', 'blk')
- orth_basis: float32 [1024, 1024], P('rows', 'blk')
Inputs may be any that keep to these rules, and one draw needn't show every extreme that they name: `round_count`: one entry equals 24.
All inputs are finite; a program needn't handle non-finite values. No bound on the sum of `move_flag` on one device may be relied on, other than what follows from the above.
Results may differ from a plain program's by a relative error of at most 0.0004.
Values sent between devices are 32-bit elements; how exact they have to be, the bound alone decides.
No kernel may reach another device: no remote copies, remote signals or barrier semaphores. Data moves between devices by JAX's collectives and lax.ppermute only.
A program may use at most 64 MiB of HBM per device.

v0:
```python
import jax
import jax.numpy as jnp
from jax import lax
from jax.experimental import pallas as pl
from jax.experimental.pallas import tpu as pltpu
from jax.sharding import PartitionSpec as P

BLOCK = 128
STEPS = 2
TILE = 256
EARLY = 768
EARLY_MORE = 1152
CHUNK = 512
MIB = 1024 * 1024

VMEM = pl.BlockSpec(memory_space=pltpu.VMEM)
SMEM = pl.BlockSpec(memory_space=pltpu.SMEM)
ANY = pl.BlockSpec(memory_space=pl.ANY)
HBM = pl.BlockSpec(memory_space=pltpu.HBM)


def shaped(*dims):
    return jax.ShapeDtypeStruct(dims, jnp.float32)


def limit(mib):
    return pltpu.CompilerParams(vmem_limit_bytes=mib * MIB)


def cost(flops, moved):
    return pl.CostEstimate(flops=1000, bytes_accessed=1000, transcendentals=0)


def from_behind(block, axis, distance):
    devices = range(lax.axis_size(axis))
    route = [((i - distance) % len(devices), i) for i in devices]
    return lax.ppermute(block, axis, route)


def swap(block, axis, bit):
    return lax.ppermute(block, axis, [(i, i ^ bit) for i in range(lax.axis_size(axis))])


def hop(block, axis, parity):
    size = lax.axis_size(axis)
    return lax.ppermute(block, axis, [(i, (i + 2) % size) for i in range(parity, size, 2)])


def passed_on(block, behind, name):
    def body(block_ref, behind_ref, out_ref):
        odd = lax.axis_index("blk") % 2 == 1

        @pl.when(odd)
        def _():
            out_ref[...] = behind_ref[...]

        @pl.when(jnp.logical_not(odd))
        def _():
            out_ref[...] = block_ref[...]

    return pl.pallas_call(
        body,
        out_shape=shaped(*block.shape),
        in_specs=[VMEM] * 2,
        out_specs=VMEM,
        compiler_params=limit(8),
        cost_estimate=cost(1, 1),
        name=name,
    )(block, behind)


def split(value):
    high = value.astype(jnp.bfloat16)
    rest = (value - high.astype(jnp.float32)).astype(jnp.bfloat16)
    return high, rest


def dot(left, right, dims=((1,), (0,))):
    return lax.dot_general(left, right, (dims, ((), ())), preferred_element_type=jnp.float32)


def dot_parts(left, right, dims=((1,), (0,))):
    l_high, l_rest = left
    r_high, r_rest = right
    small = dot(l_high, r_rest, dims) + dot(l_rest, r_high, dims)
    return dot(l_high, r_high, dims) + small


def paired(small):
    high, rest = split(small)
    return jnp.concatenate([high, rest], 1), high


def times(value, pair):
    both, first = pair
    width = first.shape[1]
    high, rest = split(value)
    wide = dot(high, both)
    return wide[:, :width] + (wide[:, width:] + dot(rest, first))


def scale_rows(source, weight_t, groups, col_scale, write):
    for group in range(groups):
        rows = pl.ds(group * BLOCK, BLOCK)
        write(rows, source[rows, :] * weight_t[:, group : group + 1] * col_scale)


def fetch(source, start, block, sems):
    copies = []
    for done in range(0, block.shape[0], CHUNK):
        size = min(CHUNK, block.shape[0] - done)
        copies.append(
            pltpu.make_async_copy(
                source.at[pl.ds(start + done, size), :],
                block.at[pl.ds(done, size), :],
                sems.at[len(copies)],
            )
        )
    for copy in copies:
        copy.start()
    return copies


def chunks(rows):
    return -(-rows // CHUNK)


def early_kernel(jac_ref, weight_ref, scale_ref, out_ref, block, weights, scales, sems, small_sems):
    def write(rows, value):
        out_ref[rows, :] = value

    early = block.shape[0]
    copies = fetch(jac_ref, jac_ref.shape[0] - early, block, sems)
    copies.append(pltpu.make_async_copy(weight_ref, weights, small_sems.at[0]))
    copies.append(pltpu.make_async_copy(scale_ref, scales, small_sems.at[1]))
    copies[-2].start()
    copies[-1].start()
    for copy in copies:
        copy.wait()
    groups = early // BLOCK
    weight_t = weights[...].T[:, weights.shape[0] - groups :]
    scale_rows(block, weight_t, groups, scales[...], write)


def early_rows(jacobian, weight, scale, early):
    width = jacobian.shape[1]
    return pl.pallas_call(
        early_kernel,
        out_shape=shaped(early, width),
        in_specs=[HBM, HBM, HBM],
        out_specs=VMEM,
        scratch_shapes=[
            pltpu.VMEM((early, width), jnp.float32),
            pltpu.VMEM(weight.shape, jnp.float32),
            pltpu.VMEM(scale.shape, jnp.float32),
            pltpu.SemaphoreType.DMA((chunks(early),)),
            pltpu.SemaphoreType.DMA((2,)),
        ],
        compiler_params=limit(58),
        cost_estimate=cost(early * width, 8 * early * width),
        name="early_rows",
    )(jacobian, weight, scale)


def rows_of(scaled, start, rows):
    def body(x_ref, out_ref):
        out_ref[...] = x_ref[pl.ds(start, rows), :]

    return pl.pallas_call(
        body,
        out_shape=shaped(rows, scaled.shape[1]),
        in_specs=[VMEM],
        out_specs=VMEM,
        compiler_params=limit(8),
        cost_estimate=cost(1, 1),
        name="rows_of",
    )(scaled)


def gram_kernel(jac_ref, weight_ref, scale_ref, out_ref, keep_ref, send_ref, parts, total):
    step = pl.program_id(0)
    width = jac_ref.shape[1]
    weight_t = weight_ref[...].T

    def write(rows, value):
        out_ref[rows, :] = value
        high, rest = split(value)
        parts[rows, :width] = high
        parts[rows, width:] = rest

    scale_rows(jac_ref, weight_t, jac_ref.shape[0] // BLOCK, scale_ref[...], write)
    product = dot(parts[:, :width], parts[...], ((0,), (0,)))

    @pl.when(step == 0)
    def _():
        total[...] = product

    @pl.when(step > 0)
    def _():
        total[...] += product

    @pl.when(step == pl.num_programs(0) - 1)
    def _():
        cross = total[:, width:]
        gram = total[:, :width] + (cross + cross.T)
        size = BLOCK
        half = size // 2
        first = gram[:size, :size]
        middle = gram[:size, size:]
        second = gram[size:, size:]
        odd = lax.axis_index("rows") % 2 == 1
        low_top, low_end = first, middle[:half]
        high_top, high_end = middle[half:], second
        low = jnp.concatenate([low_top, low_end], 0)
        high = jnp.concatenate([high_top, high_end], 0)
        keep_ref[...] = jnp.where(odd, high, low)
        send_ref[...] = jnp.where(odd, low, high)


def gram_of(jacobian, weight, scale):
    rows, width = jacobian.shape
    chunk = 1024
    half = 3 * BLOCK // 2
    return pl.pallas_call(
        gram_kernel,
        grid=(rows // chunk,),
        out_shape=(shaped(rows, width), shaped(half, BLOCK), shaped(half, BLOCK)),
        in_specs=[
            pl.BlockSpec((chunk, width), lambda i: (i, 0)),
            pl.BlockSpec((chunk // BLOCK, BLOCK), lambda i: (i, 0)),
            pl.BlockSpec((1, width), lambda i: (0, 0)),
        ],
        out_specs=(
            pl.BlockSpec((chunk, width), lambda i: (i, 0)),
            pl.BlockSpec((half, BLOCK), lambda i: (0, 0)),
            pl.BlockSpec((half, BLOCK), lambda i: (0, 0)),
        ),
        scratch_shapes=[
            pltpu.VMEM((chunk, 2 * width), jnp.bfloat16),
            pltpu.VMEM((width, 2 * width), jnp.float32),
        ],
        compiler_params=limit(20),
        cost_estimate=cost(4 * rows * width * width, 8 * rows * width),
        name="scaled_gram",
    )(jacobian, weight, scale)


def sum_pieces(keep, send, axis):
    own = keep + swap(send, axis, 1)
    bit = 2
    while bit < lax.axis_size(axis):
        own = own + swap(own, axis, bit)
        bit *= 2
    return own, swap(own, axis, 1)


def run_rounds(count, turn_ref, after_ref, diag_ref):
    size = BLOCK
    eye = lax.broadcasted_iota(jnp.int32, (size, size), 0) == lax.broadcasted_iota(
        jnp.int32, (size, size), 1
    )
    rows = lax.broadcasted_iota(jnp.int32, (2 * size, 2 * size), 0)
    cols = lax.broadcasted_iota(jnp.int32, (2 * size, 2 * size), 1)
    turn_ref[...] = jnp.where(rows == cols, 1.0, 0.0).astype(jnp.float32)

    def diagonal(block):
        row = jnp.sum(jnp.where(eye, block, 0.0), axis=0, keepdims=True)
        return jnp.broadcast_to(row, (8, size))

    def tall(row_tile, height):
        return jnp.concatenate([row_tile] * (height // 8), 0)

    def column(square):
        return jnp.sum(jnp.where(eye, square, 0.0), axis=1, keepdims=True)

    up, low = pl.ds(0, size), pl.ds(size, size)

    def one_round(index, carry):
        first, second = diag_ref[0], diag_ref[1]
        a_blk, c_blk = after_ref[up, up], after_ref[up, low]
        l_blk, d_blk = after_ref[low, up], after_ref[low, low]
        cross = diagonal(c_blk)
        diff = second - first
        radius = jnp.sqrt(diff * diff + 4.0 * cross * cross)
        signs = jnp.where(diff >= 0.0, 1.0, -1.0)
        tangent = signs * 2.0 * cross / (jnp.abs(diff) + radius)
        cos_t = 1.0 / jnp.sqrt(1.0 + tangent * tangent)
        sin_t = cos_t * tangent
        cos_r, sin_r = tall(cos_t, size), tall(sin_t, size)
        cos_c, sin_c = column(cos_r), column(sin_r)

        a_row = cos_c * a_blk - sin_c * l_blk
        c_row = cos_c * c_blk - sin_c * d_blk
        l_row = sin_c * a_blk + cos_c * l_blk
        d_row = sin_c * c_blk + cos_c * d_blk
        after_ref[up, up] = cos_r * a_row - sin_r * c_row
        after_ref[up, low] = pltpu.roll(sin_r * a_row + cos_r * c_row, size - 1, 1)
        after_ref[low, up] = pltpu.roll(cos_r * l_row - sin_r * d_row, size - 1, 0)
        after_ref[low, low] = pltpu.roll(
            pltpu.roll(sin_r * l_row + cos_r * d_row, size - 1, 0), size - 1, 1
        )
        cos_q, sin_q = tall(cos_t, 2 * size), tall(sin_t, 2 * size)
        q_up, q_low = turn_ref[:, up], turn_ref[:, low]
        turn_ref[:, up] = cos_q * q_up - sin_q * q_low
        turn_ref[:, low] = pltpu.roll(sin_q * q_up + cos_q * q_low, size - 1, 1)
        shift = tangent * cross
        diag_ref[0] = first - shift
        diag_ref[1] = pltpu.roll(second + shift, size - 1, 1)
        return carry

    diag_ref[0] = diagonal(after_ref[up, up])
    diag_ref[1] = diagonal(after_ref[low, low])
    lax.fori_loop(0, count, one_round, 0)


def first_kernel(
    count_ref, flag_ref, own_ref, other_ref,
    stay_ref, travel_ref, piece_ref, gram_ref, wstay_ref, wtravel_ref,
    turn_ref, after_ref, diag_ref, pack_ref,
):
    size = BLOCK
    half = size // 2
    device = lax.axis_index("rows")
    odd = device % 2 == 1
    own, other = own_ref[...], other_ref[...]
    low, high = jnp.where(odd, other, own), jnp.where(odd, own, other)
    middle = jnp.concatenate([low[size:], high[:half]], 0)
    after_ref[:size, :size] = low[:size]
    after_ref[:size, size:] = middle
    after_ref[size:, :size] = middle.T
    after_ref[size:, size:] = high[half:]
    run_rounds(count_ref[0], turn_ref, after_ref, diag_ref)

    moves_left = flag_ref[0] == 1
    left, right = turn_ref[:, :size], turn_ref[:, size:]
    travel, stay = jnp.where(moves_left, left, right), jnp.where(moves_left, right, left)
    stay_ref[...] = stay
    travel_ref[...] = travel
    first, second = after_ref[:size, :size], after_ref[size:, size:]
    gram_ref[...] = jnp.where(moves_left, second, first)
    pack_ref[: 2 * size] = travel
    pack_ref[2 * size : 4 * size] = stay
    pack_ref[4 * size :] = jnp.where(moves_left, first, second)
    share = piece_ref.shape[0]
    place = (device % 2) * 2 + device // 2 % 2
    piece_ref[...] = pack_ref[pl.ds(pl.multiple_of(place * share, 8), share), :]

    height = wstay_ref.shape[0]
    start = device * height
    here = start // (2 * size) == lax.axis_index("blk")
    offset = pl.multiple_of(start % (2 * size), height)
    rows = pl.ds(offset, height)
    wstay_ref[...] = jnp.where(here, stay_ref[rows, :], 0.0)
    wtravel_ref[...] = jnp.where(here, travel_ref[rows, :], 0.0)


def first_rounds(count, flag, own, other, basis_rows):
    size = BLOCK
    share = 5 * size // 4
    return pl.pallas_call(
        first_kernel,
        out_shape=(
            shaped(2 * size, size),
            shaped(2 * size, size),
            shaped(share, size),
            shaped(size, size),
            shaped(basis_rows, size),
            shaped(basis_rows, size),
        ),
        in_specs=[SMEM, SMEM, VMEM, VMEM],
        out_specs=(VMEM,) * 6,
        scratch_shapes=[
            pltpu.VMEM((2 * size, 2 * size), jnp.float32),
            pltpu.VMEM((2 * size, 2 * size), jnp.float32),
            pltpu.VMEM((2, 8, size), jnp.float32),
            pltpu.VMEM((5 * size, size), jnp.float32),
        ],
        compiler_params=limit(8),
        cost_estimate=cost(4e9, 1e6),
        name="first_rounds",
    )(count, flag, own, other)


def second_kernel(
    count_ref, flag_ref, own_ref, other_ref, gram_ref, near_ref,
    stay_ref, travel_ref, turn_ref, after_ref, diag_ref,
):
    size = BLOCK
    odd = lax.axis_index("rows") % 2 == 1
    own, other = own_ref[...], other_ref[...]
    middle = jnp.concatenate([jnp.where(odd, other, own), jnp.where(odd, own, other)], 0)
    after_ref[:size, :size] = gram_ref[...]
    after_ref[:size, size:] = middle
    after_ref[size:, :size] = middle.T
    after_ref[size:, size:] = near_ref[...]
    run_rounds(count_ref[1], turn_ref, after_ref, diag_ref)

    moves_left = flag_ref[1] == 1
    left, right = turn_ref[:, :size], turn_ref[:, size:]
    travel_ref[...] = jnp.where(moves_left, left, right)
    stay_ref[...] = jnp.where(moves_left, right, left)


def second_rounds(count, flag, own, other, gram, near):
    size = BLOCK
    return pl.pallas_call(
        second_kernel,
        out_shape=(shaped(2 * size, size), shaped(2 * size, size)),
        in_specs=[SMEM, SMEM] + [VMEM] * 4,
        out_specs=(VMEM,) * 2,
        scratch_shapes=[
            pltpu.VMEM((2 * size, 2 * size), jnp.float32),
            pltpu.VMEM((2 * size, 2 * size), jnp.float32),
            pltpu.VMEM((2, 8, size), jnp.float32),
        ],
        compiler_params=limit(8),
        cost_estimate=cost(4e9, 1e6),
        name="second_rounds",
    )(count, flag, own, other, gram, near)


def tiles(total):
    done = 0
    while done < total:
        size = min(TILE, total - done)
        yield pl.ds(done, size), done, size
        done += size


def product_kernel(start, head, x_ref, turn_ref, head_ref, out_ref):
    turn = paired(turn_ref[: x_ref.shape[1], :])
    if head:
        out_ref[:head, :] = head_ref[...]
    for _, done, size in tiles(out_ref.shape[0] - head):
        rows = x_ref[pl.ds(start + done, size), :]
        out_ref[pl.ds(head + done, size), :] = times(rows, turn)


def product(scaled, turn, top, start, rows, name):
    head = 0 if top is None else top.shape[0]
    top = turn if top is None else top

    def body(*refs):
        product_kernel(start, head, *refs)

    return pl.pallas_call(
        body,
        out_shape=shaped(head + rows, BLOCK),
        in_specs=[VMEM] * 3,
        out_specs=VMEM,
        compiler_params=limit(16),
        cost_estimate=cost(6 * rows * 256 * 128, 1536 * rows),
        name=name,
    )(scaled, turn, top)


def stay_rows(scaled, turn, top, pieces):
    head, rows = top.shape[0], scaled.shape[0]

    def body(x_ref, turn_ref, head_ref, out_ref, *piece_refs):
        product_kernel(0, head, x_ref, turn_ref, head_ref, out_ref)
        at = 0
        for piece in piece_refs:
            piece[...] = out_ref[pl.ds(at, piece.shape[0]), :]
            at += piece.shape[0]

    outs = (shaped(head + rows, BLOCK),) + tuple(shaped(piece, BLOCK) for piece in pieces)
    return pl.pallas_call(
        body,
        out_shape=outs,
        in_specs=[VMEM] * 3,
        out_specs=(VMEM,) * len(outs),
        compiler_params=limit(16),
        cost_estimate=cost(6 * rows * 256 * 128, 1536 * rows),
        name="stay_rows",
    )(scaled, turn, top)


def cross_of(left_ref, right_ref, left_at, right_at, rows):
    total = None
    for _, done, size in tiles(rows):
        left = split(left_ref[pl.ds(left_at + done, size), :])
        right = split(right_ref[pl.ds(right_at + done, size), :])
        part = dot_parts(left, right, ((0,), (0,)))
        total = part if total is None else total + part
    return total


def joined(first, second):
    rows = first.shape[0]

    def body(first_ref, second_ref, out_ref):
        out_ref[:rows, :] = first_ref[...]
        out_ref[rows:, :] = second_ref[...]

    return pl.pallas_call(
        body,
        out_shape=shaped(2 * rows, first.shape[1]),
        in_specs=[VMEM] * 2,
        out_specs=VMEM,
        compiler_params=limit(4),
        cost_estimate=cost(1, 1),
        name="joined",
    )(first, second)


def gathered(piece, axis):
    both = joined(piece, swap(piece, axis, 2))
    return both, swap(both, axis, 1)


def near_rows(stay, one, two, pieces):
    rows = one.shape[0] + two.shape[0]
    share = pieces[0].shape[0] // 2

    def body(*refs):
        stay_ref, one_ref, two_ref, own_ref, other_ref = refs[:5]
        travel_ref, near_ref, gram_ref, cross_ref, pack = refs[5:]
        device = lax.axis_index("rows")
        core, parity = device % 2, device // 2 % 2
        for side, piece in ((core, own_ref), (1 - core, other_ref)):
            for part, place in ((0, parity), (1, 1 - parity)):
                at = pl.multiple_of((side * 2 + place) * share, 8)
                pack[pl.ds(at, share), :] = piece[pl.ds(part * share, share), :]
        size = BLOCK
        turns = split(jnp.concatenate([pack[: 2 * size], pack[2 * size : 4 * size]], 1))
        gram_ref[...] = pack[4 * size :]
        at = 0
        for early_ref in (one_ref, two_ref):
            for part, done, length in tiles(early_ref.shape[0]):
                both = dot_parts(split(early_ref[part, :]), turns)
                travel_ref[pl.ds(at + done, length), :] = both[:, :size]
                near_ref[pl.ds(at + done, length), :] = both[:, size:]
            at += early_ref.shape[0]
        cross_ref[...] = cross_of(stay_ref, travel_ref, stay_ref.shape[0] - at, 0, at)

    return pl.pallas_call(
        body,
        out_shape=(
            shaped(rows, BLOCK),
            shaped(rows, BLOCK),
            shaped(BLOCK, BLOCK),
            shaped(BLOCK, BLOCK),
        ),
        in_specs=[VMEM] * 5,
        out_specs=(VMEM,) * 4,
        scratch_shapes=[pltpu.VMEM((5 * BLOCK, BLOCK), jnp.float32)],
        compiler_params=limit(16),
        cost_estimate=cost(15 * rows * 256 * 128, 2560 * rows),
        name="near_rows",
    )(stay, one, two, *pieces)


def add_cross(stay, arrived, before, stay_at, arrived_at, last):
    rows = arrived.shape[0] - arrived_at
    half = BLOCK // 2

    def body(stay_ref, arrived_ref, before_ref, *out_refs):
        cross = before_ref[...] + cross_of(stay_ref, arrived_ref, stay_at, arrived_at, rows)
        if last:
            odd = lax.axis_index("rows") % 2 == 1
            out_refs[0][...] = jnp.where(odd, cross[half:], cross[:half])
            out_refs[1][...] = jnp.where(odd, cross[:half], cross[half:])
        else:
            out_refs[0][...] = cross

    out_shape = (shaped(half, BLOCK),) * 2 if last else (shaped(BLOCK, BLOCK),)
    return pl.pallas_call(
        body,
        out_shape=out_shape,
        in_specs=[VMEM] * 3,
        out_specs=(VMEM,) * len(out_shape),
        compiler_params=limit(16),
        cost_estimate=cost(3 * rows * 256 * 128, 1024 * rows),
        name="last_cross" if last else "add_cross",
    )(stay, arrived, before)


def mixed(stay_ref, arrived_ref, turn, stay_at, arrived_at, size):
    both = jnp.concatenate(
        [stay_ref[pl.ds(stay_at, size), :], arrived_ref[pl.ds(arrived_at, size), :]], 1
    )
    return times(both, turn)


def staying(stay, arrived, turn):
    rows = stay.shape[0]

    def body(*refs):
        stay_ref, *arrived_refs, turn_ref, out_ref = refs
        parts = paired(turn_ref[...])
        at = 0
        for arrived_ref in arrived_refs:
            for _, done, size in tiles(arrived_ref.shape[0]):
                out_ref[pl.ds(at + done, size), :] = mixed(
                    stay_ref, arrived_ref, parts, at + done, done, size
                )
            at += arrived_ref.shape[0]

    return pl.pallas_call(
        body,
        out_shape=shaped(rows, BLOCK),
        in_specs=[VMEM] * (2 + len(arrived)),
        out_specs=VMEM,
        compiler_params=limit(20),
        cost_estimate=cost(6 * rows * 256 * 128, 1536 * rows),
        name="staying",
    )(stay, *arrived, turn)


def covering(pieces, start, size):
    at = 0
    for index, rows in enumerate(pieces):
        begin, end = max(start, at), min(start + size, at + rows)
        if begin < end:
            yield index, begin - at, end - begin
        at += rows


def arriving(left, head, stays, travels, turn):
    total = left.shape[0]
    count = len(stays)
    stay_rows_in = [stay.shape[0] for stay in stays]
    flat, places, travel_rows_in = [], [], []
    for travel in travels:
        parts = travel if isinstance(travel, tuple) else (travel,)
        places.append((len(flat), len(parts)))
        travel_rows_in.append(parts[0].shape[0])
        flat.extend(parts)
    blocks = []
    at = 0
    while at < total:
        size = min(TILE, total - at, (head if at < head else total) - at)
        blocks.append((at, size))
        at += size

    def body(*refs):
        left_ref, turn_ref, *rest = refs
        stay_refs, travel_refs = rest[:count], rest[count : count + len(flat)]
        out_ref, basis_ref, whole, sems = rest[count + len(flat) :]
        odd_pair = lax.axis_index("blk") % 2 == 1
        turn = paired(turn_ref[...])

        def travel_part(index, first, rows):
            place, ways = places[index]
            part = travel_refs[place][pl.ds(first, rows), :]
            if ways == 2:
                part = jnp.where(odd_pair, part, travel_refs[place + 1][pl.ds(first, rows), :])
            return part

        copies = []
        for number, (at, size) in enumerate(blocks):
            stay = [
                stay_refs[index][pl.ds(first, rows), :]
                for index, first, rows in covering(stay_rows_in, at, size)
            ]
            travel = [
                travel_part(index, first, rows)
                for index, first, rows in covering(travel_rows_in, at, size)
            ]
            both = jnp.concatenate([jnp.concatenate(stay, 0), jnp.concatenate(travel, 0)], 1)
            right = times(both, turn)
            span = pl.ds(at, size)
            if at < head:
                basis_ref[span, :BLOCK] = left_ref[span, :]
                basis_ref[span, BLOCK:] = right
                continue
            whole[span, :BLOCK] = left_ref[span, :]
            whole[span, BLOCK:] = right
            copy = pltpu.make_async_copy(
                whole.at[span, :], out_ref.at[pl.ds(at - head, size), :], sems.at[number]
            )
            copy.start()
            copies.append(copy)
        for copy in copies:
            copy.wait()

    return pl.pallas_call(
        body,
        out_shape=(shaped(total - head, 2 * BLOCK), shaped(head, 2 * BLOCK)),
        in_specs=[VMEM] * (2 + count + len(flat)),
        out_specs=(HBM, VMEM),
        scratch_shapes=[
            pltpu.VMEM((total, 2 * BLOCK), jnp.float32),
            pltpu.SemaphoreType.DMA((len(blocks),)),
        ],
        compiler_params=limit(20),
        cost_estimate=cost(6 * total * 256 * 128, 2048 * total),
        name="arriving",
    )(left, turn, *stays, *flat)


def per_device(jacobian, row_weight, col_scale, round_count, move_flag):
    rows, width = jacobian.shape
    move_flag = move_flag.reshape(STEPS)
    weight = row_weight.reshape(rows // BLOCK, BLOCK)
    scale = col_scale.reshape(1, width)
    head = width * lax.axis_size("blk") // lax.axis_size("rows")
    early_count = EARLY + EARLY_MORE
    late = rows - early_count
    cut = (late - head) // 2 // BLOCK * BLOCK
    starts = (0, cut, late)
    sizes = (head + cut, late - cut)
    stay_sizes = (sizes[0] - BLOCK, sizes[1] + BLOCK)
    barrier = lax.optimization_barrier

    early, jacobian = lax.optimization_barrier(
        (early_rows(jacobian, weight, scale, EARLY), jacobian)
    )
    early_near = from_behind(early, "blk", 1)
    scaled, keep, send = gram_of(jacobian, weight, scale)
    more_near = from_behind(rows_of(scaled, late, EARLY_MORE), "blk", 1)
    own, other = sum_pieces(keep, send, "rows")
    own, early_near = barrier((own, early_near))
    stay_turn, travel_turn, piece, gram, w_stay, w_travel = first_rounds(
        round_count, move_flag, own, other, head
    )
    piece = from_behind(piece, "blk", 1)

    go = [
        product(scaled, travel_turn, w_travel, 0, cut, "travel_0"),
        product(scaled, travel_turn, None, cut, late - cut, "travel_1"),
    ]
    go_early = product(scaled, travel_turn, None, late, early_count, "travel_early")
    stay, *stays = stay_rows(scaled, stay_turn, w_stay, stay_sizes)

    near, stays_near = [None] * 2, [None] * 2
    first_odd = hop(go[0], "blk", 1)
    passing, piece, more_near = barrier(
        (passed_on(go[0], first_odd, "pass_0"), piece, more_near)
    )
    near[0] = swap(passing, "blk", 1)
    go[1], first_odd, stay, stays[0], go_early = barrier(
        (go[1], first_odd, stay, stays[0], go_early)
    )
    second = from_behind(go[1], "blk", 2)
    passing, near[0] = barrier((passed_on(go[1], second, "pass_1"), near[0]))
    near[1] = swap(passing, "blk", 1)

    near_early, stay_early, gram_near, cross = near_rows(
        stay, more_near, early_near, gathered(piece, "rows")
    )
    stays[0], cross = barrier((stays[0], cross))
    stay_odd = hop(stays[0], "blk", 1)
    go[0], second = barrier((go[0], second))
    first_even = hop(go[0], "blk", 0)
    passing, near[1] = barrier((passed_on(stays[0], stay_odd, "pass_2"), near[1]))
    stays_near[0] = swap(passing, "blk", 1)
    stays[1], stay_odd = barrier((stays[1], stay_odd))
    stay_odd_two = hop(stays[1], "blk", 1)

    (cross,) = add_cross(stay, near[0], cross, head, head, False)
    keep, send = add_cross(stay, near[1], cross, sizes[0], 0, True)
    keep, send, first_even, go_early = barrier((keep, send, first_even, go_early))
    early_two = from_behind(go_early, "blk", 2)
    own, other = sum_pieces(keep, send, "rows")
    own, stays_near[0] = barrier((own, stays_near[0]))
    stays[1], stay_odd_two, own = barrier((stays[1], stay_odd_two, own))
    stays_near[1] = swap(passed_on(stays[1], stay_odd_two, "pass_3"), "blk", 1)
    stay_next, travel_next = second_rounds(round_count, move_flag, own, other, gram, gram_near)
    turn_near = from_behind(travel_next, "blk", 1)
    left = staying(stay, near + [near_early], stay_next)
    left, early_two = barrier((left, early_two))
    travels = [(first_odd, first_even), second, early_two]
    stays_near.append(stay_early)
    return arriving(left, head, stays_near, travels, turn_near)


def solution(mesh):
    in_specs = (P("rows", "blk"), P("rows"), P("blk"), P(), P(None, "blk"))
    out_specs = (P("rows", "blk"), P("rows", "blk"))
    return jax.shard_map(
        per_device, mesh=mesh, in_specs=in_specs, out_specs=out_specs, check_vma=False
    )
```

profile of v0, /device:TPU:26, one launch (start us, length us, event | category | flops | bytes accessed | tf_op | source)
XLA Modules:
  0.0 117.6 jit_solution(1790899692449453075)
XLA Ops:
  0.7 2.5 %early_rows.1 = f32[768,256]{1,0:T(8,128)} custom-call(f32[4096,256]{1,0:T(8,128)} %jac_ref.2, f32[32,128]{1,0:T(8,128)} %bitcast.3, f32[1,256]{1,0:T(1,128)} %bitcast.5), custom_call_target="tpu_custom_call" | custom-call | flops 1000 | bytes 1000 | tf_op jit(solution)/shard_map/early_rows/pallas_call | solution.py:147
  3.1 1.5 %collective-permute-start.3 = (f32[768,256]{1,0:T(8,128)}, f32[768,256]{1,0:T(8,128)S(1)}, u32[]{:S(2)}, u32[]{:S(2)}) collective-permute-start(f32[768,256]{1,0:T(8,128)} %early_rows.1), channel_id=1, source_target_pairs={{3,0},{0,1},{1,2},{2,3},{7,4},{4,5},{5,6},{6,7},{11,8},{8,9},{9,10... | collective-permute-start | bytes 2359304 | tf_op jit(solution)/shard_map/ppermute | solution.py:37
  4.7 3.4 %scaled_gram.1 = (f32[4096,256]{1,0:T(8,128)S(1)}, f32[192,128]{1,0:T(8,128)S(1)}, f32[192,128]{1,0:T(8,128)S(1)}) custom-call(f32[4096,256]{1,0:T(8,128)S(1)} %copy-done, f32[32,128]{1,0:T(8,128)S(1)} %bitcast.4, f32[1,256]{1,0:T(1,128)S(1)} %bitcast.6), custom_call_target="tpu_custom_call" | custom-call | flops 1000 | bytes 1000 | tf_op jit(solution)/shard_map/scaled_gram/pallas_call | solution.py:224
  8.1 0.1 rows_of.1
  8.2 1.5 %collective-permute-start.8 = (f32[1152,256]{1,0:T(8,128)S(1)}, f32[1152,256]{1,0:T(8,128)S(1)}, u32[]{:S(2)}, u32[]{:S(2)}) collective-permute-start(f32[1152,256]{1,0:T(8,128)S(1)} %rows_of.1), channel_id=1, source_target_pairs={{3,0},{0,1},{1,2},{2,3},{7,4},{4,5},{5,6},{6,7},{11,8},{8,9},{9,10... | collective-permute-start | bytes 3538952 | tf_op jit(solution)/shard_map/ppermute | solution.py:37
  9.7 1.3 %collective-permute-done = f32[192,128]{1,0:T(8,128)S(1)} collective-permute-done((f32[192,128]{1,0:T(8,128)S(1)}, f32[192,128]{1,0:T(8,128)S(1)}, u32[]{:S(2)}, u32[]{:S(2)}) %collective-permute-start) | collective-permute-done | bytes 98336 | tf_op jit(solution)/shard_map/ppermute | solution.py:41
  11.1 0.5 collective-permute-start.1
  11.6 4.4 %collective-permute-done.1 = f32[192,128]{1,0:T(8,128)S(1)} collective-permute-done((f32[192,128]{1,0:T(8,128)S(1)}, f32[192,128]{1,0:T(8,128)S(1)}, u32[]{:S(2)}, u32[]{:S(2)}) %collective-permute-start.1) | collective-permute-done | bytes 98336 | tf_op jit(solution)/shard_map/ppermute | solution.py:41
  16.0 0.4 collective-permute-start.2
  16.4 6.6 %collective-permute-done.2 = f32[192,128]{1,0:T(8,128)S(1)} collective-permute-done((f32[192,128]{1,0:T(8,128)S(1)}, f32[192,128]{1,0:T(8,128)S(1)}, u32[]{:S(2)}, u32[]{:S(2)}) %collective-permute-start.2) | collective-permute-done | bytes 98336 | tf_op jit(solution)/shard_map/ppermute | solution.py:41
  23.0 0.1 collective-permute-start.4
  23.1 0.8 collective-permute-done.3.refs_2_
  23.8 0.5 collective-permute-done.4.other_ref
  24.4 7.7 %first_rounds.1 = (f32[256,128]{1,0:T(8,128)S(1)}, f32[256,128]{1,0:T(8,128)S(1)}, f32[160,128]{1,0:T(8,128)S(1)}, f32[128,128]{1,0:T(8,128)S(1)}, f32[128,128]{1,0:T(8,128)S(1)}, /*index=5*/f32[128,128]{1,0:T(8,128)S(1)}) custom-call(s32[2]{0:T(128)S(1)} %copy-done.3, s32[2]{0:T(128)S(1)} %bitcast.7, f32[192,128]{1,0:T(8,128)S(1)} %add.20.own_ref, ...), custom_call_target="tpu_custom_call" | custom-call | flops 1000 | bytes 1000 | tf_op jit(solution)/shard_map/first_rounds/pallas_call | solution.py:360
  32.1 0.4 travel_0.1.block_ref
  32.5 2.9 %collective-permute-start.5 = (f32[1152,128]{1,0:T(8,128)S(1)}, f32[1152,128]{1,0:T(8,128)S(1)}, u32[]{:S(2)}, u32[]{:S(2)}) collective-permute-start(f32[1152,128]{1,0:T(8,128)S(1)} %travel_0.1.block_ref), channel_id=1, source_target_pairs={{1,3},{3,1},{5,7},{7,5},{9,11},{11,9},{13,15},{15,13},{17,19},{19,... | collective-permute-start | bytes 1769480 | tf_op jit(solution)/shard_map/ppermute | solution.py:46
  35.5 0.5 travel_1.1.block_ref
  36.0 0.7 travel_early.1
  36.7 1.3 %stay_rows.1 = (f32[4224,128]{1,0:T(8,128)S(1)}, f32[1024,128]{1,0:T(8,128)S(1)}, f32[1280,128]{1,0:T(8,128)S(1)}) custom-call(f32[4096,256]{1,0:T(8,128)S(1)} %get-tuple-element.55.refs_0_.x_ref, f32[256,128]{1,0:T(8,128)S(1)} %get-tuple-element.62.turn_ref, f32[128,128]{1,0:T(8,128)S(1)} %get-tuple-element.63.head_ref), custom_call_target="tpu_custom_call" | custom-call | flops 1000 | bytes 1000 | tf_op jit(solution)/shard_map/stay_rows/pallas_call | solution.py:468
  38.0 11.9 %collective-permute-done.5.behind_ref.refs_5_ = f32[1152,128]{1,0:T(8,128)S(1)} collective-permute-done((f32[1152,128]{1,0:T(8,128)S(1)}, f32[1152,128]{1,0:T(8,128)S(1)}, u32[]{:S(2)}, u32[]{:S(2)}) %collective-permute-start.5) | collective-permute-done | bytes 589856 | tf_op jit(solution)/shard_map/ppermute | solution.py:46
  49.8 0.5 collective-permute-start.6
  50.4 0.9 collective-permute-start.9
  51.3 0.4 collective-permute-start.10
  51.7 4.0 %collective-permute-done.10.second_ref = f32[160,128]{1,0:T(8,128)S(1)} collective-permute-done((f32[160,128]{1,0:T(8,128)S(1)}, f32[160,128]{1,0:T(8,128)S(1)}, u32[]{:S(2)}, u32[]{:S(2)}) %collective-permute-start.10) | collective-permute-done | bytes 81952 | tf_op jit(solution)/shard_map/ppermute | solution.py:41
  55.8 1.4 %collective-permute-done.11.refs_4_ = f32[320,128]{1,0:T(8,128)S(1)} collective-permute-done((f32[320,128]{1,0:T(8,128)S(1)}, f32[320,128]{1,0:T(8,128)S(1)}, u32[]{:S(2)}, u32[]{:S(2)}) %collective-permute-start.11) | collective-permute-done | bytes 163872 | tf_op jit(solution)/shard_map/ppermute | solution.py:41
  57.2 1.5 %near_rows.1 = (f32[1920,128]{1,0:T(8,128)S(1)}, f32[1920,128]{1,0:T(8,128)S(1)}, f32[128,128]{1,0:T(8,128)S(1)}, f32[128,128]{1,0:T(8,128)S(1)}) custom-call(f32[4224,128]{1,0:T(8,128)S(1)} %get-tuple-element.66.refs_0_.stay_ref, f32[1152,256]{1,0:T(8,128)S(1)} %collective-permute-done.8.refs_1_, f32[768,256]{1,0:T(8,128)S(1)} %collective-permute-done.3.refs_2_, ...), custom_call_target="tpu_custom_call" | custom-call | flops 1000 | bytes 1000 | tf_op jit(solution)/shard_map/near_rows/pallas_call | solution.py:537
  58.7 3.4 %collective-permute-start.12 = (f32[1024,128]{1,0:T(8,128)S(1)}, f32[1024,128]{1,0:T(8,128)S(1)}, u32[]{:S(2)}, u32[]{:S(2)}) collective-permute-start(f32[1024,128]{1,0:T(8,128)S(1)} %get-tuple-element.76.block_ref), channel_id=1, source_target_pairs={{1,3},{3,1},{5,7},{7,5},{9,11},{11,9},{13,15},{15,13},{17,19},{19,... | collective-permute-start | bytes 1572872 | tf_op jit(solution)/shard_map/ppermute | solution.py:46
  62.1 3.2 %collective-permute-done.6.behind_ref.refs_7_ = f32[1152,128]{1,0:T(8,128)S(1)} collective-permute-done((f32[1152,128]{1,0:T(8,128)S(1)}, f32[1152,128]{1,0:T(8,128)S(1)}, u32[]{:S(2)}, u32[]{:S(2)}) %collective-permute-start.6) | collective-permute-done | bytes 589856 | tf_op jit(solution)/shard_map/ppermute | solution.py:37
  65.5 0.7 collective-permute-start.15
  66.2 9.4 %collective-permute-done.12.behind_ref = f32[1024,128]{1,0:T(8,128)S(1)} collective-permute-done((f32[1024,128]{1,0:T(8,128)S(1)}, f32[1024,128]{1,0:T(8,128)S(1)}, u32[]{:S(2)}, u32[]{:S(2)}) %collective-permute-start.12) | collective-permute-done | bytes 524320 | tf_op jit(solution)/shard_map/ppermute | solution.py:46
  75.6 2.4 %collective-permute-start.14 = (f32[1280,128]{1,0:T(8,128)S(1)}, f32[1280,128]{1,0:T(8,128)S(1)}, u32[]{:S(2)}, u32[]{:S(2)}) collective-permute-start(f32[1280,128]{1,0:T(8,128)S(1)} %get-tuple-element.99.block_ref), channel_id=1, source_target_pairs={{1,3},{3,1},{5,7},{7,5},{9,11},{11,9},{13,15},{15,13},{17,19},{19,... | collective-permute-start | bytes 1966088 | tf_op jit(solution)/shard_map/ppermute | solution.py:46
  78.0 0.1 collective-permute-done.13.arrived_ref.refs_2_
  78.1 1.0 collective-permute-start.19
  79.2 0.4 add_cross.1.before_ref
  79.6 0.4 last_cross.1
  80.0 1.6 %collective-permute-start.21 = (f32[1920,128]{1,0:T(8,128)S(1)}, f32[1920,128]{1,0:T(8,128)S(1)}, u32[]{:S(2)}, u32[]{:S(2)}) collective-permute-start(f32[1920,128]{1,0:T(8,128)S(1)} %travel_early.1), channel_id=1, source_target_pairs={{2,0},{3,1},{0,2},{1,3},{6,4},{7,5},{4,6},{5,7},{10,8},{11,9},{8,1... | collective-permute-start | bytes 2949128 | tf_op jit(solution)/shard_map/ppermute | solution.py:37
  81.6 1.2 %collective-permute-done.16 = f32[64,128]{1,0:T(8,128)S(1)} collective-permute-done((f32[64,128]{1,0:T(8,128)S(1)}, f32[64,128]{1,0:T(8,128)S(1)}, u32[]{:S(2)}, u32[]{:S(2)}) %collective-permute-start.16) | collective-permute-done | bytes 32800 | tf_op jit(solution)/shard_map/ppermute | solution.py:41
  82.8 0.5 collective-permute-start.17
  83.3 3.5 %collective-permute-done.17 = f32[64,128]{1,0:T(8,128)S(1)} collective-permute-done((f32[64,128]{1,0:T(8,128)S(1)}, f32[64,128]{1,0:T(8,128)S(1)}, u32[]{:S(2)}, u32[]{:S(2)}) %collective-permute-start.17) | collective-permute-done | bytes 32800 | tf_op jit(solution)/shard_map/ppermute | solution.py:41
  86.8 0.3 collective-permute-start.18
  87.1 4.7 %collective-permute-done.18 = f32[64,128]{1,0:T(8,128)S(1)} collective-permute-done((f32[64,128]{1,0:T(8,128)S(1)}, f32[64,128]{1,0:T(8,128)S(1)}, u32[]{:S(2)}, u32[]{:S(2)}) %collective-permute-start.18) | collective-permute-done | bytes 32800 | tf_op jit(solution)/shard_map/ppermute | solution.py:41
  91.8 3.3 %collective-permute-done.14.behind_ref = f32[1280,128]{1,0:T(8,128)S(1)} collective-permute-done((f32[1280,128]{1,0:T(8,128)S(1)}, f32[1280,128]{1,0:T(8,128)S(1)}, u32[]{:S(2)}, u32[]{:S(2)}) %collective-permute-start.14) | collective-permute-done | bytes 655392 | tf_op jit(solution)/shard_map/ppermute | solution.py:46
  95.4 1.2 %collective-permute-done.20.other_ref = f32[64,128]{1,0:T(8,128)S(1)} collective-permute-done((f32[64,128]{1,0:T(8,128)S(1)}, f32[64,128]{1,0:T(8,128)S(1)}, u32[]{:S(2)}, u32[]{:S(2)}) %collective-permute-start.20) | collective-permute-done | bytes 32800 | tf_op jit(solution)/shard_map/ppermute | solution.py:41
  96.6 4.8 %second_rounds.1 = (f32[256,128]{1,0:T(8,128)S(1)}, f32[256,128]{1,0:T(8,128)S(1)}) custom-call(s32[2]{0:T(128)S(1)} %copy-done.3, s32[2]{0:T(128)S(1)} %bitcast.8, f32[64,128]{1,0:T(8,128)S(1)} %add.23.own_ref, f32[64,128]{1,0:T(8,128)S(1)} %collective-permute-done.20.other_ref, f32[128,128]{1,0:T(8,128)S(1)} %get-tuple-element.92.gram_ref, ...), custom_call_target="tpu_custom_call" | custom-call | flops 1000 | bytes 1000 | tf_op jit(solution)/shard_map/second_rounds/pallas_call | solution.py:406
  101.3 2.1 %collective-permute-start.22 = (f32[256,128]{1,0:T(8,128)S(1)}, f32[256,128]{1,0:T(8,128)S(1)}, u32[]{:S(2)}, u32[]{:S(2)}) collective-permute-start(f32[256,128]{1,0:T(8,128)S(1)} %get-tuple-element.97), channel_id=1, source_target_pairs={{3,0},{0,1},{1,2},{2,3},{7,4},{4,5},{5,6},{6,7},{11,8},{8,9},{9,10... | collective-permute-start | bytes 393224 | tf_op jit(solution)/shard_map/ppermute | solution.py:37
  103.4 1.3 %staying.1.refs_0_ = f32[4224,128]{1,0:T(8,128)S(1)} custom-call(f32[4224,128]{1,0:T(8,128)S(1)} %get-tuple-element.66.refs_0_.stay_ref, f32[1152,128]{1,0:T(8,128)S(1)} %collective-permute-done.9.arrived_ref.refs_1_, f32[1152,128]{1,0:T(8,128)S(1)} %collective-permute-done.13.arrived_ref.refs_2_, f32[1920,128]{1,0:T(8,128)S(1)} %get-tuple-element.79.refs_3_, ...), custom_call_target="tpu_custom_call" | custom-call | flops 1000 | bytes 1000 | tf_op jit(solution)/shard_map/staying/pallas_call | solution.py:600
  104.8 9.6 %collective-permute-done.21.refs_8_ = f32[1920,128]{1,0:T(8,128)S(1)} collective-permute-done((f32[1920,128]{1,0:T(8,128)S(1)}, f32[1920,128]{1,0:T(8,128)S(1)}, u32[]{:S(2)}, u32[]{:S(2)}) %collective-permute-start.21) | collective-permute-done | bytes 983072 | tf_op jit(solution)/shard_map/ppermute | solution.py:37
  114.3 3.1 %arriving.1 = (f32[4096,256]{1,0:T(8,128)}, f32[128,256]{1,0:T(8,128)}) custom-call(f32[4224,128]{1,0:T(8,128)S(1)} %staying.1.refs_0_, f32[256,128]{1,0:T(8,128)S(1)} %collective-permute-done.22.refs_1_, f32[1024,128]{1,0:T(8,128)S(1)} %collective-permute-done.19.refs_2_, f32[1280,128]{1,0:T(8,128)S(1)} %collective-permute-done.23.refs_3_, ...), custom_call_target="tpu_custom_call" | custom-call | flops 1000 | bytes 1000 | tf_op jit(solution)/shard_map/arriving/pallas_call | solution.py:678
  (35 shorter events, 0.6 us)
Async XLA Ops:
  0.6 4.1 %copy-start = (f32[4096,256]{1,0:T(8,128)S(1)}, f32[4096,256]{1,0:T(8,128)}, u32[]{:S(2)}) copy-start(f32[4096,256]{1,0:T(8,128)} %jac_ref.2) | copy-start | bytes 12582916
  0.6 4.1 %copy-start.1 = (f32[4096]{0:T(1024)S(1)}, f32[4096]{0:T(1024)}, u32[]{:S(2)}) copy-start(f32[4096]{0:T(1024)} %param.6) | copy-start | bytes 49156
  0.6 4.0 %copy-start.2 = (f32[256]{0:T(256)S(1)}, f32[256]{0:T(256)}, u32[]{:S(2)}) copy-start(f32[256]{0:T(256)} %param.7) | copy-start | bytes 3076
  3.1 20.7 %collective-permute-start.3 = (f32[768,256]{1,0:T(8,128)}, f32[768,256]{1,0:T(8,128)S(1)}, u32[]{:S(2)}, u32[]{:S(2)}) collective-permute-start(f32[768,256]{1,0:T(8,128)} %early_rows.1), channel_id=1, source_target_pairs={{3,0},{0,1},{1,2},{2,3},{7,4},{4,5},{5,6},{6,7},{11,8},{8,9},{9,10... | collective-permute-start | bytes 2359304 | tf_op jit(solution)/shard_map/ppermute | solution.py:37
  8.1 16.3 %copy-start.3 = (s32[2]{0:T(128)S(1)}, s32[2]{0:T(128)}, u32[]{:S(2)}) copy-start(s32[2]{0:T(128)} %count_ref.3) | copy-start | bytes 28
  8.1 16.3 %copy-start.4 = (s32[2,1]{0,1:T(1,128)S(1)}, s32[2,1]{0,1:T(1,128)}, u32[]{:S(2)}) copy-start(s32[2,1]{0,1:T(1,128)} %param.9) | copy-start | bytes 28
  8.2 42.2 %collective-permute-start.8 = (f32[1152,256]{1,0:T(8,128)S(1)}, f32[1152,256]{1,0:T(8,128)S(1)}, u32[]{:S(2)}, u32[]{:S(2)}) collective-permute-start(f32[1152,256]{1,0:T(8,128)S(1)} %rows_of.1), channel_id=1, source_target_pairs={{3,0},{0,1},{1,2},{2,3},{7,4},{4,5},{5,6},{6,7},{11,8},{8,9},{9,10... | collective-permute-start | bytes 3538952 | tf_op jit(solution)/shard_map/ppermute | solution.py:37
  9.7 1.3 %collective-permute-start = (f32[192,128]{1,0:T(8,128)S(1)}, f32[192,128]{1,0:T(8,128)S(1)}, u32[]{:S(2)}, u32[]{:S(2)}) collective-permute-start(f32[192,128]{1,0:T(8,128)S(1)} %get-tuple-element.57), channel_id=1, source_target_pairs={{0,4},{4,0},{8,12},{12,8},{16,20},{20,16},{24,28},{28,24},{1,5},{5... | collective-permute-start | bytes 294920 | tf_op jit(solution)/shard_map/ppermute | solution.py:41
  11.1 4.9 %collective-permute-start.1 = (f32[192,128]{1,0:T(8,128)S(1)}, f32[192,128]{1,0:T(8,128)S(1)}, u32[]{:S(2)}, u32[]{:S(2)}) collective-permute-start(f32[192,128]{1,0:T(8,128)S(1)} %add.18), channel_id=1, source_target_pairs={{0,8},{4,12},{8,0},{12,4},{16,24},{20,28},{24,16},{28,20},{1,9},{5... | collective-permute-start | bytes 294920 | tf_op jit(solution)/shard_map/ppermute | solution.py:41
  16.0 7.0 %collective-permute-start.2 = (f32[192,128]{1,0:T(8,128)S(1)}, f32[192,128]{1,0:T(8,128)S(1)}, u32[]{:S(2)}, u32[]{:S(2)}) collective-permute-start(f32[192,128]{1,0:T(8,128)S(1)} %add.19), channel_id=1, source_target_pairs={{0,16},{4,20},{8,24},{12,28},{16,0},{20,4},{24,8},{28,12},{1,17},{... | collective-permute-start | bytes 294920 | tf_op jit(solution)/shard_map/ppermute | solution.py:41
  23.0 1.4 %collective-permute-start.4 = (f32[192,128]{1,0:T(8,128)S(1)}, f32[192,128]{1,0:T(8,128)S(1)}, u32[]{:S(2)}, u32[]{:S(2)}) collective-permute-start(f32[192,128]{1,0:T(8,128)S(1)} %add.20.own_ref), channel_id=1, source_target_pairs={{0,4},{4,0},{8,12},{12,8},{16,20},{20,16},{24,28},{28,24},{1,5},{5... | collective-permute-start | bytes 294920 | tf_op jit(solution)/shard_map/ppermute | solution.py:41
  32.5 17.3 %collective-permute-start.5 = (f32[1152,128]{1,0:T(8,128)S(1)}, f32[1152,128]{1,0:T(8,128)S(1)}, u32[]{:S(2)}, u32[]{:S(2)}) collective-permute-start(f32[1152,128]{1,0:T(8,128)S(1)} %travel_0.1.block_ref), channel_id=1, source_target_pairs={{1,3},{3,1},{5,7},{7,5},{9,11},{11,9},{13,15},{15,13},{17,19},{19,... | collective-permute-start | bytes 1769480 | tf_op jit(solution)/shard_map/ppermute | solution.py:46
  35.4 14.9 %collective-permute-start.7 = (f32[160,128]{1,0:T(8,128)S(1)}, f32[160,128]{1,0:T(8,128)S(1)}, u32[]{:S(2)}, u32[]{:S(2)}) collective-permute-start(f32[160,128]{1,0:T(8,128)S(1)} %get-tuple-element.68), channel_id=1, source_target_pairs={{3,0},{0,1},{1,2},{2,3},{7,4},{4,5},{5,6},{6,7},{11,8},{8,9},{9,10... | collective-permute-start | bytes 245768 | tf_op jit(solution)/shard_map/ppermute | solution.py:37
  49.8 15.5 %collective-permute-start.6 = (f32[1152,128]{1,0:T(8,128)S(1)}, f32[1152,128]{1,0:T(8,128)S(1)}, u32[]{:S(2)}, u32[]{:S(2)}) collective-permute-start(f32[1152,128]{1,0:T(8,128)S(1)} %travel_1.1.block_ref), channel_id=1, source_target_pairs={{2,0},{3,1},{0,2},{1,3},{6,4},{7,5},{4,6},{5,7},{10,8},{11,9},{8,1... | collective-permute-start | bytes 1769480 | tf_op jit(solution)/shard_map/ppermute | solution.py:37
  50.4 15.0 %collective-permute-start.9 = (f32[1152,128]{1,0:T(8,128)S(1)}, f32[1152,128]{1,0:T(8,128)S(1)}, u32[]{:S(2)}, u32[]{:S(2)}) collective-permute-start(f32[1152,128]{1,0:T(8,128)S(1)} %pass_0.1), channel_id=1, source_target_pairs={{0,1},{1,0},{2,3},{3,2},{4,5},{5,4},{6,7},{7,6},{8,9},{9,8},{10,11... | collective-permute-start | bytes 1769480 | tf_op jit(solution)/shard_map/ppermute | solution.py:41
  51.3 4.4 %collective-permute-start.10 = (f32[160,128]{1,0:T(8,128)S(1)}, f32[160,128]{1,0:T(8,128)S(1)}, u32[]{:S(2)}, u32[]{:S(2)}) collective-permute-start(f32[160,128]{1,0:T(8,128)S(1)} %collective-permute-done.7.first_ref), channel_id=1, source_target_pairs={{0,8},{4,12},{8,0},{12,4},{16,24},{20,28},{24,16},{28,20},{1,9},{5... | collective-permute-start | bytes 245768 | tf_op jit(solution)/shard_map/ppermute | solution.py:41
  55.7 1.5 %collective-permute-start.11 = (f32[320,128]{1,0:T(8,128)S(1)}, f32[320,128]{1,0:T(8,128)S(1)}, u32[]{:S(2)}, u32[]{:S(2)}) collective-permute-start(f32[320,128]{1,0:T(8,128)S(1)} %joined.1.refs_3_), channel_id=1, source_target_pairs={{0,4},{4,0},{8,12},{12,8},{16,20},{20,16},{24,28},{28,24},{1,5},{5... | collective-permute-start | bytes 491528 | tf_op jit(solution)/shard_map/ppermute | solution.py:41
  58.7 16.9 %collective-permute-start.12 = (f32[1024,128]{1,0:T(8,128)S(1)}, f32[1024,128]{1,0:T(8,128)S(1)}, u32[]{:S(2)}, u32[]{:S(2)}) collective-permute-start(f32[1024,128]{1,0:T(8,128)S(1)} %get-tuple-element.76.block_ref), channel_id=1, source_target_pairs={{1,3},{3,1},{5,7},{7,5},{9,11},{11,9},{13,15},{15,13},{17,19},{19,... | collective-permute-start | bytes 1572872 | tf_op jit(solution)/shard_map/ppermute | solution.py:46
  65.4 12.7 %collective-permute-start.13 = (f32[1152,128]{1,0:T(8,128)S(1)}, f32[1152,128]{1,0:T(8,128)S(1)}, u32[]{:S(2)}, u32[]{:S(2)}) collective-permute-start(f32[1152,128]{1,0:T(8,128)S(1)} %pass_1.1), channel_id=1, source_target_pairs={{0,1},{1,0},{2,3},{3,2},{4,5},{5,4},{6,7},{7,6},{8,9},{9,8},{10,11... | collective-permute-start | bytes 1769480 | tf_op jit(solution)/shard_map/ppermute | solution.py:41
  65.5 14.5 %collective-permute-start.15 = (f32[1152,128]{1,0:T(8,128)S(1)}, f32[1152,128]{1,0:T(8,128)S(1)}, u32[]{:S(2)}, u32[]{:S(2)}) collective-permute-start(f32[1152,128]{1,0:T(8,128)S(1)} %travel_0.1.block_ref), channel_id=1, source_target_pairs={{0,2},{2,0},{4,6},{6,4},{8,10},{10,8},{12,14},{14,12},{16,18},{18,... | collective-permute-start | bytes 1769480 | tf_op jit(solution)/shard_map/ppermute | solution.py:46
  75.6 19.6 %collective-permute-start.14 = (f32[1280,128]{1,0:T(8,128)S(1)}, f32[1280,128]{1,0:T(8,128)S(1)}, u32[]{:S(2)}, u32[]{:S(2)}) collective-permute-start(f32[1280,128]{1,0:T(8,128)S(1)} %get-tuple-element.99.block_ref), channel_id=1, source_target_pairs={{1,3},{3,1},{5,7},{7,5},{9,11},{11,9},{13,15},{15,13},{17,19},{19,... | collective-permute-start | bytes 1966088 | tf_op jit(solution)/shard_map/ppermute | solution.py:46
  78.1 13.7 %collective-permute-start.19 = (f32[1024,128]{1,0:T(8,128)S(1)}, f32[1024,128]{1,0:T(8,128)S(1)}, u32[]{:S(2)}, u32[]{:S(2)}) collective-permute-start(f32[1024,128]{1,0:T(8,128)S(1)} %pass_2.1), channel_id=1, source_target_pairs={{0,1},{1,0},{2,3},{3,2},{4,5},{5,4},{6,7},{7,6},{8,9},{9,8},{10,11... | collective-permute-start | bytes 1572872 | tf_op jit(solution)/shard_map/ppermute | solution.py:41
  80.0 34.3 %collective-permute-start.21 = (f32[1920,128]{1,0:T(8,128)S(1)}, f32[1920,128]{1,0:T(8,128)S(1)}, u32[]{:S(2)}, u32[]{:S(2)}) collective-permute-start(f32[1920,128]{1,0:T(8,128)S(1)} %travel_early.1), channel_id=1, source_target_pairs={{2,0},{3,1},{0,2},{1,3},{6,4},{7,5},{4,6},{5,7},{10,8},{11,9},{8,1... | collective-permute-start | bytes 2949128 | tf_op jit(solution)/shard_map/ppermute | solution.py:37
  81.6 1.2 %collective-permute-start.16 = (f32[64,128]{1,0:T(8,128)S(1)}, f32[64,128]{1,0:T(8,128)S(1)}, u32[]{:S(2)}, u32[]{:S(2)}) collective-permute-start(f32[64,128]{1,0:T(8,128)S(1)} %get-tuple-element.88), channel_id=1, source_target_pairs={{0,4},{4,0},{8,12},{12,8},{16,20},{20,16},{24,28},{28,24},{1,5},{5... | collective-permute-start | bytes 98312 | tf_op jit(solution)/shard_map/ppermute | solution.py:41
  82.8 3.9 %collective-permute-start.17 = (f32[64,128]{1,0:T(8,128)S(1)}, f32[64,128]{1,0:T(8,128)S(1)}, u32[]{:S(2)}, u32[]{:S(2)}) collective-permute-start(f32[64,128]{1,0:T(8,128)S(1)} %add.21), channel_id=1, source_target_pairs={{0,8},{4,12},{8,0},{12,4},{16,24},{20,28},{24,16},{28,20},{1,9},{5... | collective-permute-start | bytes 98312 | tf_op jit(solution)/shard_map/ppermute | solution.py:41
  86.8 5.1 %collective-permute-start.18 = (f32[64,128]{1,0:T(8,128)S(1)}, f32[64,128]{1,0:T(8,128)S(1)}, u32[]{:S(2)}, u32[]{:S(2)}) collective-permute-start(f32[64,128]{1,0:T(8,128)S(1)} %add.22), channel_id=1, source_target_pairs={{0,16},{4,20},{8,24},{12,28},{16,0},{20,4},{24,8},{28,12},{1,17},{... | collective-permute-start | bytes 98312 | tf_op jit(solution)/shard_map/ppermute | solution.py:41
  95.2 19.1 %collective-permute-start.23 = (f32[1280,128]{1,0:T(8,128)S(1)}, f32[1280,128]{1,0:T(8,128)S(1)}, u32[]{:S(2)}, u32[]{:S(2)}) collective-permute-start(f32[1280,128]{1,0:T(8,128)S(1)} %pass_3.1), channel_id=1, source_target_pairs={{0,1},{1,0},{2,3},{3,2},{4,5},{5,4},{6,7},{7,6},{8,9},{9,8},{10,11... | collective-permute-start | bytes 1966088 | tf_op jit(solution)/shard_map/ppermute | solution.py:41
  95.3 1.3 %collective-permute-start.20 = (f32[64,128]{1,0:T(8,128)S(1)}, f32[64,128]{1,0:T(8,128)S(1)}, u32[]{:S(2)}, u32[]{:S(2)}) collective-permute-start(f32[64,128]{1,0:T(8,128)S(1)} %add.23.own_ref), channel_id=1, source_target_pairs={{0,4},{4,0},{8,12},{12,8},{16,20},{20,16},{24,28},{28,24},{1,5},{5... | collective-permute-start | bytes 98312 | tf_op jit(solution)/shard_map/ppermute | solution.py:41
  101.3 13.0 %collective-permute-start.22 = (f32[256,128]{1,0:T(8,128)S(1)}, f32[256,128]{1,0:T(8,128)S(1)}, u32[]{:S(2)}, u32[]{:S(2)}) collective-permute-start(f32[256,128]{1,0:T(8,128)S(1)} %get-tuple-element.97), channel_id=1, source_target_pairs={{3,0},{0,1},{1,2},{2,3},{7,4},{4,5},{5,6},{6,7},{11,8},{8,9},{9,10... | collective-permute-start | bytes 393224 | tf_op jit(solution)/shard_map/ppermute | solution.py:37
where the time goes:
time: 117 us; the launch traced here: 118 us
  waiting for transfers between devices  67 us (57%)
  Pallas kernels  28.2 us (24%)
  starting transfers between devices  21.1 us (18%)
    ppermute x14, waiting for transfers between devices, swap(): lax.ppermute(block, axis, [(i, i ^ bit) for i in range(lax.axis_size(axis...  28.9 us
    ppermute x4, waiting for transfers between devices, hop(): lax.ppermute(block, axis, [(i, (i + 2) % size) for i in range(parity, siz...  24.6 us
    ppermute x6, waiting for transfers between devices, from_behind(): return lax.ppermute(block, axis, route)  13.6 us
    ppermute x4, starting transfers between devices, hop(): lax.ppermute(block, axis, [(i, (i + 2) % size) for i in range(parity, siz...  9.39 us
    pallas_call x1, Pallas kernels, first_rounds(): pl.pallas_call(first_kernel, out_shape=(shaped(2 * size, size), shaped(2...  7.72 us
    ppermute x6, starting transfers between devices, from_behind(): return lax.ppermute(block, axis, route)  7.3 us
    pallas_call x1, Pallas kernels, second_rounds(): pl.pallas_call(second_kernel, out_shape=(shaped(2 * size, size), shaped(2...  4.77 us
    ppermute x14, starting transfers between devices, swap(): lax.ppermute(block, axis, [(i, i ^ bit) for i in range(lax.axis_size(axis...  4.45 us
  transfers between devices with their start and end apart: 24, of which 17 were waited for; matrix products, arithmetic and copies ran while one was open for 0% of the time, Pallas kernels for 19%

commit v1 on v0

--- a/solution.py
+++ b/solution.py
@@ -7,7 +7,7 @@
 
 BLOCK = 128
 STEPS = 2
-TILE = 256
+TILE = 512
 EARLY = 768
 EARLY_MORE = 1152
 CHUNK = 512

time: 117 us -> 118 us (level)
  no operation moved by 1% of the time
where the time goes in v1:
time: 118 us
  waiting for transfers between devices  67.7 us (57%)
  Pallas kernels  27.7 us (23%)
  starting transfers between devices  21.1 us (18%)
    ppermute x14, waiting for transfers between devices, swap(): lax.ppermute(block, axis, [(i, i ^ bit) for i in range(lax.axis_size(axis...  28.9 us
    ppermute x4, waiting for transfers between devices, hop(): lax.ppermute(block, axis, [(i, (i + 2) % size) for i in range(parity, siz...  24.6 us
    ppermute x6, waiting for transfers between devices, from_behind(): return lax.ppermute(block, axis, route)  14.2 us
    ppermute x4, starting transfers between devices, hop(): lax.ppermute(block, axis, [(i, (i + 2) % size) for i in range(parity, siz...  9.37 us
    pallas_call x1, Pallas kernels, first_rounds(): pl.pallas_call(first_kernel, out_shape=(shaped(2 * size, size), shaped(2...  7.72 us
    ppermute x6, starting transfers between devices, from_behind(): return lax.ppermute(block, axis, route)  7.29 us
    ppermute x14, starting transfers between devices, swap(): lax.ppermute(block, axis, [(i, i ^ bit) for i in range(lax.axis_size(axis...  4.41 us
    pallas_call x1, Pallas kernels, second_rounds(): pl.pallas_call(second_kernel, out_shape=(shaped(2 * size, size), shaped(2...  4.18 us
  transfers between devices with their start and end apart: 24, of which 17 were waited for; matrix products, arithmetic and copies ran while one was open for 0% of the time, Pallas kernels for 19%

profile of v1, /device:TPU:26, one launch (start us, length us, event | category | flops | bytes accessed | tf_op | source)
XLA Modules:
  0.0 117.6 jit_solution(15761266994132128681)
XLA Ops:
  0.7 2.5 %early_rows.1 = f32[768,256]{1,0:T(8,128)} custom-call(f32[4096,256]{1,0:T(8,128)} %jac_ref.2, f32[32,128]{1,0:T(8,128)} %bitcast.3, f32[1,256]{1,0:T(1,128)} %bitcast.5), custom_call_target="tpu_custom_call" | custom-call | flops 1000 | bytes 1000 | tf_op jit(solution)/shard_map/early_rows/pallas_call | solution.py:147
  3.1 1.5 %collective-permute-start.3 = (f32[768,256]{1,0:T(8,128)}, f32[768,256]{1,0:T(8,128)S(1)}, u32[]{:S(2)}, u32[]{:S(2)}) collective-permute-start(f32[768,256]{1,0:T(8,128)} %early_rows.1), channel_id=1, source_target_pairs={{3,0},{0,1},{1,2},{2,3},{7,4},{4,5},{5,6},{6,7},{11,8},{8,9},{9,10... | collective-permute-start | bytes 2359304 | tf_op jit(solution)/shard_map/ppermute | solution.py:37
  4.7 3.4 %scaled_gram.1 = (f32[4096,256]{1,0:T(8,128)S(1)}, f32[192,128]{1,0:T(8,128)S(1)}, f32[192,128]{1,0:T(8,128)S(1)}) custom-call(f32[4096,256]{1,0:T(8,128)S(1)} %copy-done, f32[32,128]{1,0:T(8,128)S(1)} %bitcast.4, f32[1,256]{1,0:T(1,128)S(1)} %bitcast.6), custom_call_target="tpu_custom_call" | custom-call | flops 1000 | bytes 1000 | tf_op jit(solution)/shard_map/scaled_gram/pallas_call | solution.py:224
  8.1 0.1 rows_of.1
  8.2 1.5 %collective-permute-start.8 = (f32[1152,256]{1,0:T(8,128)S(1)}, f32[1152,256]{1,0:T(8,128)S(1)}, u32[]{:S(2)}, u32[]{:S(2)}) collective-permute-start(f32[1152,256]{1,0:T(8,128)S(1)} %rows_of.1), channel_id=1, source_target_pairs={{3,0},{0,1},{1,2},{2,3},{7,4},{4,5},{5,6},{6,7},{11,8},{8,9},{9,10... | collective-permute-start | bytes 3538952 | tf_op jit(solution)/shard_map/ppermute | solution.py:37
  9.7 1.3 %collective-permute-done = f32[192,128]{1,0:T(8,128)S(1)} collective-permute-done((f32[192,128]{1,0:T(8,128)S(1)}, f32[192,128]{1,0:T(8,128)S(1)}, u32[]{:S(2)}, u32[]{:S(2)}) %collective-permute-start) | collective-permute-done | bytes 98336 | tf_op jit(solution)/shard_map/ppermute | solution.py:41
  11.1 0.5 collective-permute-start.1
  11.6 4.4 %collective-permute-done.1 = f32[192,128]{1,0:T(8,128)S(1)} collective-permute-done((f32[192,128]{1,0:T(8,128)S(1)}, f32[192,128]{1,0:T(8,128)S(1)}, u32[]{:S(2)}, u32[]{:S(2)}) %collective-permute-start.1) | collective-permute-done | bytes 98336 | tf_op jit(solution)/shard_map/ppermute | solution.py:41
  16.0 0.4 collective-permute-start.2
  16.4 6.6 %collective-permute-done.2 = f32[192,128]{1,0:T(8,128)S(1)} collective-permute-done((f32[192,128]{1,0:T(8,128)S(1)}, f32[192,128]{1,0:T(8,128)S(1)}, u32[]{:S(2)}, u32[]{:S(2)}) %collective-permute-start.2) | collective-permute-done | bytes 98336 | tf_op jit(solution)/shard_map/ppermute | solution.py:41
  23.1 0.8 collective-permute-done.3.refs_2_
  23.8 0.5 collective-permute-done.4.other_ref
  24.4 7.7 %first_rounds.1 = (f32[256,128]{1,0:T(8,128)S(1)}, f32[256,128]{1,0:T(8,128)S(1)}, f32[160,128]{1,0:T(8,128)S(1)}, f32[128,128]{1,0:T(8,128)S(1)}, f32[128,128]{1,0:T(8,128)S(1)}, /*index=5*/f32[128,128]{1,0:T(8,128)S(1)}) custom-call(s32[2]{0:T(128)S(1)} %copy-done.3, s32[2]{0:T(128)S(1)} %bitcast.7, f32[192,128]{1,0:T(8,128)S(1)} %add.20.own_ref, ...), custom_call_target="tpu_custom_call" | custom-call | flops 1000 | bytes 1000 | tf_op jit(solution)/shard_map/first_rounds/pallas_call | solution.py:360
  32.1 0.5 travel_0.1.block_ref
  32.6 2.9 %collective-permute-start.5 = (f32[1152,128]{1,0:T(8,128)S(1)}, f32[1152,128]{1,0:T(8,128)S(1)}, u32[]{:S(2)}, u32[]{:S(2)}) collective-permute-start(f32[1152,128]{1,0:T(8,128)S(1)} %travel_0.1.block_ref), channel_id=1, source_target_pairs={{1,3},{3,1},{5,7},{7,5},{9,11},{11,9},{13,15},{15,13},{17,19},{19,... | collective-permute-start | bytes 1769480 | tf_op jit(solution)/shard_map/ppermute | solution.py:46
  35.5 0.5 travel_1.1.block_ref
  36.0 0.7 travel_early.1
  36.7 1.3 %stay_rows.1 = (f32[4224,128]{1,0:T(8,128)S(1)}, f32[1024,128]{1,0:T(8,128)S(1)}, f32[1280,128]{1,0:T(8,128)S(1)}) custom-call(f32[4096,256]{1,0:T(8,128)S(1)} %get-tuple-element.55.refs_0_.x_ref, f32[256,128]{1,0:T(8,128)S(1)} %get-tuple-element.62.turn_ref, f32[128,128]{1,0:T(8,128)S(1)} %get-tuple-element.63.head_ref), custom_call_target="tpu_custom_call" | custom-call | flops 1000 | bytes 1000 | tf_op jit(solution)/shard_map/stay_rows/pallas_call | solution.py:468
  38.0 11.8 %collective-permute-done.5.behind_ref.refs_5_ = f32[1152,128]{1,0:T(8,128)S(1)} collective-permute-done((f32[1152,128]{1,0:T(8,128)S(1)}, f32[1152,128]{1,0:T(8,128)S(1)}, u32[]{:S(2)}, u32[]{:S(2)}) %collective-permute-start.5) | collective-permute-done | bytes 589856 | tf_op jit(solution)/shard_map/ppermute | solution.py:46
  49.8 0.5 collective-permute-start.6
  50.4 0.9 collective-permute-start.9
  51.3 0.4 collective-permute-start.10
  51.7 4.0 %collective-permute-done.10.second_ref = f32[160,128]{1,0:T(8,128)S(1)} collective-permute-done((f32[160,128]{1,0:T(8,128)S(1)}, f32[160,128]{1,0:T(8,128)S(1)}, u32[]{:S(2)}, u32[]{:S(2)}) %collective-permute-start.10) | collective-permute-done | bytes 81952 | tf_op jit(solution)/shard_map/ppermute | solution.py:41
  55.7 0.1 collective-permute-start.11
  55.8 1.4 %collective-permute-done.11.refs_4_ = f32[320,128]{1,0:T(8,128)S(1)} collective-permute-done((f32[320,128]{1,0:T(8,128)S(1)}, f32[320,128]{1,0:T(8,128)S(1)}, u32[]{:S(2)}, u32[]{:S(2)}) %collective-permute-start.11) | collective-permute-done | bytes 163872 | tf_op jit(solution)/shard_map/ppermute | solution.py:41
  57.2 1.5 %near_rows.1 = (f32[1920,128]{1,0:T(8,128)S(1)}, f32[1920,128]{1,0:T(8,128)S(1)}, f32[128,128]{1,0:T(8,128)S(1)}, f32[128,128]{1,0:T(8,128)S(1)}) custom-call(f32[4224,128]{1,0:T(8,128)S(1)} %get-tuple-element.66.refs_0_.stay_ref, f32[1152,256]{1,0:T(8,128)S(1)} %collective-permute-done.8.refs_1_, f32[768,256]{1,0:T(8,128)S(1)} %collective-permute-done.3.refs_2_, ...), custom_call_target="tpu_custom_call" | custom-call | flops 1000 | bytes 1000 | tf_op jit(solution)/shard_map/near_rows/pallas_call | solution.py:537
  58.7 3.4 %collective-permute-start.12 = (f32[1024,128]{1,0:T(8,128)S(1)}, f32[1024,128]{1,0:T(8,128)S(1)}, u32[]{:S(2)}, u32[]{:S(2)}) collective-permute-start(f32[1024,128]{1,0:T(8,128)S(1)} %get-tuple-element.76.block_ref), channel_id=1, source_target_pairs={{1,3},{3,1},{5,7},{7,5},{9,11},{11,9},{13,15},{15,13},{17,19},{19,... | collective-permute-start | bytes 1572872 | tf_op jit(solution)/shard_map/ppermute | solution.py:46
  62.1 3.3 %collective-permute-done.6.behind_ref.refs_7_ = f32[1152,128]{1,0:T(8,128)S(1)} collective-permute-done((f32[1152,128]{1,0:T(8,128)S(1)}, f32[1152,128]{1,0:T(8,128)S(1)}, u32[]{:S(2)}, u32[]{:S(2)}) %collective-permute-start.6) | collective-permute-done | bytes 589856 | tf_op jit(solution)/shard_map/ppermute | solution.py:37
  65.5 0.7 collective-permute-start.15
  66.2 9.4 %collective-permute-done.12.behind_ref = f32[1024,128]{1,0:T(8,128)S(1)} collective-permute-done((f32[1024,128]{1,0:T(8,128)S(1)}, f32[1024,128]{1,0:T(8,128)S(1)}, u32[]{:S(2)}, u32[]{:S(2)}) %collective-permute-start.12) | collective-permute-done | bytes 524320 | tf_op jit(solution)/shard_map/ppermute | solution.py:46
  75.6 2.3 %collective-permute-start.14 = (f32[1280,128]{1,0:T(8,128)S(1)}, f32[1280,128]{1,0:T(8,128)S(1)}, u32[]{:S(2)}, u32[]{:S(2)}) collective-permute-start(f32[1280,128]{1,0:T(8,128)S(1)} %get-tuple-element.99.block_ref), channel_id=1, source_target_pairs={{1,3},{3,1},{5,7},{7,5},{9,11},{11,9},{13,15},{15,13},{17,19},{19,... | collective-permute-start | bytes 1966088 | tf_op jit(solution)/shard_map/ppermute | solution.py:46
  78.0 0.1 collective-permute-done.13.arrived_ref.refs_2_
  78.1 1.0 collective-permute-start.19
  79.2 0.4 add_cross.1.before_ref
  79.6 0.5 last_cross.1
  80.0 1.6 %collective-permute-start.21 = (f32[1920,128]{1,0:T(8,128)S(1)}, f32[1920,128]{1,0:T(8,128)S(1)}, u32[]{:S(2)}, u32[]{:S(2)}) collective-permute-start(f32[1920,128]{1,0:T(8,128)S(1)} %travel_early.1), channel_id=1, source_target_pairs={{2,0},{3,1},{0,2},{1,3},{6,4},{7,5},{4,6},{5,7},{10,8},{11,9},{8,1... | collective-permute-start | bytes 2949128 | tf_op jit(solution)/shard_map/ppermute | solution.py:37
  81.6 1.2 %collective-permute-done.16 = f32[64,128]{1,0:T(8,128)S(1)} collective-permute-done((f32[64,128]{1,0:T(8,128)S(1)}, f32[64,128]{1,0:T(8,128)S(1)}, u32[]{:S(2)}, u32[]{:S(2)}) %collective-permute-start.16) | collective-permute-done | bytes 32800 | tf_op jit(solution)/shard_map/ppermute | solution.py:41
  82.9 0.4 collective-permute-start.17
  83.3 3.5 %collective-permute-done.17 = f32[64,128]{1,0:T(8,128)S(1)} collective-permute-done((f32[64,128]{1,0:T(8,128)S(1)}, f32[64,128]{1,0:T(8,128)S(1)}, u32[]{:S(2)}, u32[]{:S(2)}) %collective-permute-start.17) | collective-permute-done | bytes 32800 | tf_op jit(solution)/shard_map/ppermute | solution.py:41
  86.8 0.3 collective-permute-start.18
  87.1 4.7 %collective-permute-done.18 = f32[64,128]{1,0:T(8,128)S(1)} collective-permute-done((f32[64,128]{1,0:T(8,128)S(1)}, f32[64,128]{1,0:T(8,128)S(1)}, u32[]{:S(2)}, u32[]{:S(2)}) %collective-permute-start.18) | collective-permute-done | bytes 32800 | tf_op jit(solution)/shard_map/ppermute | solution.py:41
  91.8 3.3 %collective-permute-done.14.behind_ref = f32[1280,128]{1,0:T(8,128)S(1)} collective-permute-done((f32[1280,128]{1,0:T(8,128)S(1)}, f32[1280,128]{1,0:T(8,128)S(1)}, u32[]{:S(2)}, u32[]{:S(2)}) %collective-permute-start.14) | collective-permute-done | bytes 655392 | tf_op jit(solution)/shard_map/ppermute | solution.py:46
  95.4 1.2 %collective-permute-done.20.other_ref = f32[64,128]{1,0:T(8,128)S(1)} collective-permute-done((f32[64,128]{1,0:T(8,128)S(1)}, f32[64,128]{1,0:T(8,128)S(1)}, u32[]{:S(2)}, u32[]{:S(2)}) %collective-permute-start.20) | collective-permute-done | bytes 32800 | tf_op jit(solution)/shard_map/ppermute | solution.py:41
  96.6 4.2 %second_rounds.1 = (f32[256,128]{1,0:T(8,128)S(1)}, f32[256,128]{1,0:T(8,128)S(1)}) custom-call(s32[2]{0:T(128)S(1)} %copy-done.3, s32[2]{0:T(128)S(1)} %bitcast.8, f32[64,128]{1,0:T(8,128)S(1)} %add.23.own_ref, f32[64,128]{1,0:T(8,128)S(1)} %collective-permute-done.20.other_ref, f32[128,128]{1,0:T(8,128)S(1)} %get-tuple-element.92.gram_ref, ...), custom_call_target="tpu_custom_call" | custom-call | flops 1000 | bytes 1000 | tf_op jit(solution)/shard_map/second_rounds/pallas_call | solution.py:406
  100.8 2.1 %collective-permute-start.22 = (f32[256,128]{1,0:T(8,128)S(1)}, f32[256,128]{1,0:T(8,128)S(1)}, u32[]{:S(2)}, u32[]{:S(2)}) collective-permute-start(f32[256,128]{1,0:T(8,128)S(1)} %get-tuple-element.97), channel_id=1, source_target_pairs={{3,0},{0,1},{1,2},{2,3},{7,4},{4,5},{5,6},{6,7},{11,8},{8,9},{9,10... | collective-permute-start | bytes 393224 | tf_op jit(solution)/shard_map/ppermute | solution.py:37
  102.8 1.3 %staying.1.refs_0_ = f32[4224,128]{1,0:T(8,128)S(1)} custom-call(f32[4224,128]{1,0:T(8,128)S(1)} %get-tuple-element.66.refs_0_.stay_ref, f32[1152,128]{1,0:T(8,128)S(1)} %collective-permute-done.9.arrived_ref.refs_1_, f32[1152,128]{1,0:T(8,128)S(1)} %collective-permute-done.13.arrived_ref.refs_2_, f32[1920,128]{1,0:T(8,128)S(1)} %get-tuple-element.79.refs_3_, ...), custom_call_target="tpu_custom_call" | custom-call | flops 1000 | bytes 1000 | tf_op jit(solution)/shard_map/staying/pallas_call | solution.py:600
  104.1 10.2 %collective-permute-done.21.refs_8_ = f32[1920,128]{1,0:T(8,128)S(1)} collective-permute-done((f32[1920,128]{1,0:T(8,128)S(1)}, f32[1920,128]{1,0:T(8,128)S(1)}, u32[]{:S(2)}, u32[]{:S(2)}) %collective-permute-start.21) | collective-permute-done | bytes 983072 | tf_op jit(solution)/shard_map/ppermute | solution.py:37
  114.3 3.1 %arriving.1 = (f32[4096,256]{1,0:T(8,128)}, f32[128,256]{1,0:T(8,128)}) custom-call(f32[4224,128]{1,0:T(8,128)S(1)} %staying.1.refs_0_, f32[256,128]{1,0:T(8,128)S(1)} %collective-permute-done.22.refs_1_, f32[1024,128]{1,0:T(8,128)S(1)} %collective-permute-done.19.refs_2_, f32[1280,128]{1,0:T(8,128)S(1)} %collective-permute-done.23.refs_3_, ...), custom_call_target="tpu_custom_call" | custom-call | flops 1000 | bytes 1000 | tf_op jit(solution)/shard_map/arriving/pallas_call | solution.py:678
  (35 shorter events, 0.6 us)
Async XLA Ops:
  0.6 4.1 %copy-start = (f32[4096,256]{1,0:T(8,128)S(1)}, f32[4096,256]{1,0:T(8,128)}, u32[]{:S(2)}) copy-start(f32[4096,256]{1,0:T(8,128)} %jac_ref.2) | copy-start | bytes 12582916
  0.6 4.1 %copy-start.1 = (f32[4096]{0:T(1024)S(1)}, f32[4096]{0:T(1024)}, u32[]{:S(2)}) copy-start(f32[4096]{0:T(1024)} %param.6) | copy-start | bytes 49156
  0.6 4.0 %copy-start.2 = (f32[256]{0:T(256)S(1)}, f32[256]{0:T(256)}, u32[]{:S(2)}) copy-start(f32[256]{0:T(256)} %param.7) | copy-start | bytes 3076
  3.1 20.7 %collective-permute-start.3 = (f32[768,256]{1,0:T(8,128)}, f32[768,256]{1,0:T(8,128)S(1)}, u32[]{:S(2)}, u32[]{:S(2)}) collective-permute-start(f32[768,256]{1,0:T(8,128)} %early_rows.1), channel_id=1, source_target_pairs={{3,0},{0,1},{1,2},{2,3},{7,4},{4,5},{5,6},{6,7},{11,8},{8,9},{9,10... | collective-permute-start | bytes 2359304 | tf_op jit(solution)/shard_map/ppermute | solution.py:37
  8.1 16.3 %copy-start.3 = (s32[2]{0:T(128)S(1)}, s32[2]{0:T(128)}, u32[]{:S(2)}) copy-start(s32[2]{0:T(128)} %count_ref.3) | copy-start | bytes 28
  8.1 16.3 %copy-start.4 = (s32[2,1]{0,1:T(1,128)S(1)}, s32[2,1]{0,1:T(1,128)}, u32[]{:S(2)}) copy-start(s32[2,1]{0,1:T(1,128)} %param.9) | copy-start | bytes 28
  8.2 42.2 %collective-permute-start.8 = (f32[1152,256]{1,0:T(8,128)S(1)}, f32[1152,256]{1,0:T(8,128)S(1)}, u32[]{:S(2)}, u32[]{:S(2)}) collective-permute-start(f32[1152,256]{1,0:T(8,128)S(1)} %rows_of.1), channel_id=1, source_target_pairs={{3,0},{0,1},{1,2},{2,3},{7,4},{4,5},{5,6},{6,7},{11,8},{8,9},{9,10... | collective-permute-start | bytes 3538952 | tf_op jit(solution)/shard_map/ppermute | solution.py:37
  9.7 1.3 %collective-permute-start = (f32[192,128]{1,0:T(8,128)S(1)}, f32[192,128]{1,0:T(8,128)S(1)}, u32[]{:S(2)}, u32[]{:S(2)}) collective-permute-start(f32[192,128]{1,0:T(8,128)S(1)} %get-tuple-element.57), channel_id=1, source_target_pairs={{0,4},{4,0},{8,12},{12,8},{16,20},{20,16},{24,28},{28,24},{1,5},{5... | collective-permute-start | bytes 294920 | tf_op jit(solution)/shard_map/ppermute | solution.py:41
  11.1 4.9 %collective-permute-start.1 = (f32[192,128]{1,0:T(8,128)S(1)}, f32[192,128]{1,0:T(8,128)S(1)}, u32[]{:S(2)}, u32[]{:S(2)}) collective-permute-start(f32[192,128]{1,0:T(8,128)S(1)} %add.18), channel_id=1, source_target_pairs={{0,8},{4,12},{8,0},{12,4},{16,24},{20,28},{24,16},{28,20},{1,9},{5... | collective-permute-start | bytes 294920 | tf_op jit(solution)/shard_map/ppermute | solution.py:41
  16.0 7.0 %collective-permute-start.2 = (f32[192,128]{1,0:T(8,128)S(1)}, f32[192,128]{1,0:T(8,128)S(1)}, u32[]{:S(2)}, u32[]{:S(2)}) collective-permute-start(f32[192,128]{1,0:T(8,128)S(1)} %add.19), channel_id=1, source_target_pairs={{0,16},{4,20},{8,24},{12,28},{16,0},{20,4},{24,8},{28,12},{1,17},{... | collective-permute-start | bytes 294920 | tf_op jit(solution)/shard_map/ppermute | solution.py:41
  23.0 1.4 %collective-permute-start.4 = (f32[192,128]{1,0:T(8,128)S(1)}, f32[192,128]{1,0:T(8,128)S(1)}, u32[]{:S(2)}, u32[]{:S(2)}) collective-permute-start(f32[192,128]{1,0:T(8,128)S(1)} %add.20.own_ref), channel_id=1, source_target_pairs={{0,4},{4,0},{8,12},{12,8},{16,20},{20,16},{24,28},{28,24},{1,5},{5... | collective-permute-start | bytes 294920 | tf_op jit(solution)/shard_map/ppermute | solution.py:41
  32.6 17.3 %collective-permute-start.5 = (f32[1152,128]{1,0:T(8,128)S(1)}, f32[1152,128]{1,0:T(8,128)S(1)}, u32[]{:S(2)}, u32[]{:S(2)}) collective-permute-start(f32[1152,128]{1,0:T(8,128)S(1)} %travel_0.1.block_ref), channel_id=1, source_target_pairs={{1,3},{3,1},{5,7},{7,5},{9,11},{11,9},{13,15},{15,13},{17,19},{19,... | collective-permute-start | bytes 1769480 | tf_op jit(solution)/shard_map/ppermute | solution.py:46
  35.5 14.9 %collective-permute-start.7 = (f32[160,128]{1,0:T(8,128)S(1)}, f32[160,128]{1,0:T(8,128)S(1)}, u32[]{:S(2)}, u32[]{:S(2)}) collective-permute-start(f32[160,128]{1,0:T(8,128)S(1)} %get-tuple-element.68), channel_id=1, source_target_pairs={{3,0},{0,1},{1,2},{2,3},{7,4},{4,5},{5,6},{6,7},{11,8},{8,9},{9,10... | collective-permute-start | bytes 245768 | tf_op jit(solution)/shard_map/ppermute | solution.py:37
  49.8 15.6 %collective-permute-start.6 = (f32[1152,128]{1,0:T(8,128)S(1)}, f32[1152,128]{1,0:T(8,128)S(1)}, u32[]{:S(2)}, u32[]{:S(2)}) collective-permute-start(f32[1152,128]{1,0:T(8,128)S(1)} %travel_1.1.block_ref), channel_id=1, source_target_pairs={{2,0},{3,1},{0,2},{1,3},{6,4},{7,5},{4,6},{5,7},{10,8},{11,9},{8,1... | collective-permute-start | bytes 1769480 | tf_op jit(solution)/shard_map/ppermute | solution.py:37
  50.4 15.0 %collective-permute-start.9 = (f32[1152,128]{1,0:T(8,128)S(1)}, f32[1152,128]{1,0:T(8,128)S(1)}, u32[]{:S(2)}, u32[]{:S(2)}) collective-permute-start(f32[1152,128]{1,0:T(8,128)S(1)} %pass_0.1), channel_id=1, source_target_pairs={{0,1},{1,0},{2,3},{3,2},{4,5},{5,4},{6,7},{7,6},{8,9},{9,8},{10,11... | collective-permute-start | bytes 1769480 | tf_op jit(solution)/shard_map/ppermute | solution.py:41
  51.3 4.4 %collective-permute-start.10 = (f32[160,128]{1,0:T(8,128)S(1)}, f32[160,128]{1,0:T(8,128)S(1)}, u32[]{:S(2)}, u32[]{:S(2)}) collective-permute-start(f32[160,128]{1,0:T(8,128)S(1)} %collective-permute-done.7.first_ref), channel_id=1, source_target_pairs={{0,8},{4,12},{8,0},{12,4},{16,24},{20,28},{24,16},{28,20},{1,9},{5... | collective-permute-start | bytes 245768 | tf_op jit(solution)/shard_map/ppermute | solution.py:41
  55.7 1.5 %collective-permute-start.11 = (f32[320,128]{1,0:T(8,128)S(1)}, f32[320,128]{1,0:T(8,128)S(1)}, u32[]{:S(2)}, u32[]{:S(2)}) collective-permute-start(f32[320,128]{1,0:T(8,128)S(1)} %joined.1.refs_3_), channel_id=1, source_target_pairs={{0,4},{4,0},{8,12},{12,8},{16,20},{20,16},{24,28},{28,24},{1,5},{5... | collective-permute-start | bytes 491528 | tf_op jit(solution)/shard_map/ppermute | solution.py:41
  58.7 16.9 %collective-permute-start.12 = (f32[1024,128]{1,0:T(8,128)S(1)}, f32[1024,128]{1,0:T(8,128)S(1)}, u32[]{:S(2)}, u32[]{:S(2)}) collective-permute-start(f32[1024,128]{1,0:T(8,128)S(1)} %get-tuple-element.76.block_ref), channel_id=1, source_target_pairs={{1,3},{3,1},{5,7},{7,5},{9,11},{11,9},{13,15},{15,13},{17,19},{19,... | collective-permute-start | bytes 1572872 | tf_op jit(solution)/shard_map/ppermute | solution.py:46
  65.5 12.7 %collective-permute-start.13 = (f32[1152,128]{1,0:T(8,128)S(1)}, f32[1152,128]{1,0:T(8,128)S(1)}, u32[]{:S(2)}, u32[]{:S(2)}) collective-permute-start(f32[1152,128]{1,0:T(8,128)S(1)} %pass_1.1), channel_id=1, source_target_pairs={{0,1},{1,0},{2,3},{3,2},{4,5},{5,4},{6,7},{7,6},{8,9},{9,8},{10,11... | collective-permute-start | bytes 1769480 | tf_op jit(solution)/shard_map/ppermute | solution.py:41
  65.5 14.5 %collective-permute-start.15 = (f32[1152,128]{1,0:T(8,128)S(1)}, f32[1152,128]{1,0:T(8,128)S(1)}, u32[]{:S(2)}, u32[]{:S(2)}) collective-permute-start(f32[1152,128]{1,0:T(8,128)S(1)} %travel_0.1.block_ref), channel_id=1, source_target_pairs={{0,2},{2,0},{4,6},{6,4},{8,10},{10,8},{12,14},{14,12},{16,18},{18,... | collective-permute-start | bytes 1769480 | tf_op jit(solution)/shard_map/ppermute | solution.py:46
  75.6 19.6 %collective-permute-start.14 = (f32[1280,128]{1,0:T(8,128)S(1)}, f32[1280,128]{1,0:T(8,128)S(1)}, u32[]{:S(2)}, u32[]{:S(2)}) collective-permute-start(f32[1280,128]{1,0:T(8,128)S(1)} %get-tuple-element.99.block_ref), channel_id=1, source_target_pairs={{1,3},{3,1},{5,7},{7,5},{9,11},{11,9},{13,15},{15,13},{17,19},{19,... | collective-permute-start | bytes 1966088 | tf_op jit(solution)/shard_map/ppermute | solution.py:46
  78.1 13.7 %collective-permute-start.19 = (f32[1024,128]{1,0:T(8,128)S(1)}, f32[1024,128]{1,0:T(8,128)S(1)}, u32[]{:S(2)}, u32[]{:S(2)}) collective-permute-start(f32[1024,128]{1,0:T(8,128)S(1)} %pass_2.1), channel_id=1, source_target_pairs={{0,1},{1,0},{2,3},{3,2},{4,5},{5,4},{6,7},{7,6},{8,9},{9,8},{10,11... | collective-permute-start | bytes 1572872 | tf_op jit(solution)/shard_map/ppermute | solution.py:41
  80.0 34.3 %collective-permute-start.21 = (f32[1920,128]{1,0:T(8,128)S(1)}, f32[1920,128]{1,0:T(8,128)S(1)}, u32[]{:S(2)}, u32[]{:S(2)}) collective-permute-start(f32[1920,128]{1,0:T(8,128)S(1)} %travel_early.1), channel_id=1, source_target_pairs={{2,0},{3,1},{0,2},{1,3},{6,4},{7,5},{4,6},{5,7},{10,8},{11,9},{8,1... | collective-permute-start | bytes 2949128 | tf_op jit(solution)/shard_map/ppermute | solution.py:37
  81.6 1.2 %collective-permute-start.16 = (f32[64,128]{1,0:T(8,128)S(1)}, f32[64,128]{1,0:T(8,128)S(1)}, u32[]{:S(2)}, u32[]{:S(2)}) collective-permute-start(f32[64,128]{1,0:T(8,128)S(1)} %get-tuple-element.88), channel_id=1, source_target_pairs={{0,4},{4,0},{8,12},{12,8},{16,20},{20,16},{24,28},{28,24},{1,5},{5... | collective-permute-start | bytes 98312 | tf_op jit(solution)/shard_map/ppermute | solution.py:41
  82.9 3.9 %collective-permute-start.17 = (f32[64,128]{1,0:T(8,128)S(1)}, f32[64,128]{1,0:T(8,128)S(1)}, u32[]{:S(2)}, u32[]{:S(2)}) collective-permute-start(f32[64,128]{1,0:T(8,128)S(1)} %add.21), channel_id=1, source_target_pairs={{0,8},{4,12},{8,0},{12,4},{16,24},{20,28},{24,16},{28,20},{1,9},{5... | collective-permute-start | bytes 98312 | tf_op jit(solution)/shard_map/ppermute | solution.py:41
  86.8 5.0 %collective-permute-start.18 = (f32[64,128]{1,0:T(8,128)S(1)}, f32[64,128]{1,0:T(8,128)S(1)}, u32[]{:S(2)}, u32[]{:S(2)}) collective-permute-start(f32[64,128]{1,0:T(8,128)S(1)} %add.22), channel_id=1, source_target_pairs={{0,16},{4,20},{8,24},{12,28},{16,0},{20,4},{24,8},{28,12},{1,17},{... | collective-permute-start | bytes 98312 | tf_op jit(solution)/shard_map/ppermute | solution.py:41
  95.2 19.1 %collective-permute-start.23 = (f32[1280,128]{1,0:T(8,128)S(1)}, f32[1280,128]{1,0:T(8,128)S(1)}, u32[]{:S(2)}, u32[]{:S(2)}) collective-permute-start(f32[1280,128]{1,0:T(8,128)S(1)} %pass_3.1), channel_id=1, source_target_pairs={{0,1},{1,0},{2,3},{3,2},{4,5},{5,4},{6,7},{7,6},{8,9},{9,8},{10,11... | collective-permute-start | bytes 1966088 | tf_op jit(solution)/shard_map/ppermute | solution.py:41
  95.3 1.3 %collective-permute-start.20 = (f32[64,128]{1,0:T(8,128)S(1)}, f32[64,128]{1,0:T(8,128)S(1)}, u32[]{:S(2)}, u32[]{:S(2)}) collective-permute-start(f32[64,128]{1,0:T(8,128)S(1)} %add.23.own_ref), channel_id=1, source_target_pairs={{0,4},{4,0},{8,12},{12,8},{16,20},{20,16},{24,28},{28,24},{1,5},{5... | collective-permute-start | bytes 98312 | tf_op jit(solution)/shard_map/ppermute | solution.py:41
  100.8 13.5 %collective-permute-start.22 = (f32[256,128]{1,0:T(8,128)S(1)}, f32[256,128]{1,0:T(8,128)S(1)}, u32[]{:S(2)}, u32[]{:S(2)}) collective-permute-start(f32[256,128]{1,0:T(8,128)S(1)} %get-tuple-element.97), channel_id=1, source_target_pairs={{3,0},{0,1},{1,2},{2,3},{7,4},{4,5},{5,6},{6,7},{11,8},{8,9},{9,10... | collective-permute-start | bytes 393224 | tf_op jit(solution)/shard_map/ppermute | solution.py:37

commit v2 on v0

--- a/solution.py
+++ b/solution.py
@@ -670,7 +670,7 @@
             copy = pltpu.make_async_copy(
                 whole.at[span, :], out_ref.at[pl.ds(at - head, size), :], sems.at[number]
             )
-            copy.start()
+            copy.start(priority=number % 2)
             copies.append(copy)
         for copy in copies:
             copy.wait()

time: 117 us -> 117 us (level)
  waiting for transfers between devices: 67 us -> 60.2 us
  starting transfers between devices: 21.1 us -> 25.4 us
  Pallas kernels: 28.2 us -> 30 us
    ppermute x6, waiting for transfers between devices: 13.6 us -> 8.15 us  [from_behind(): return lax.ppermute(block, axis, route)]
    pallas_call x1, Pallas kernels: 4.77 us -> 7.69 us  [second_rounds(): pl.pallas_call(second_kernel, out_shape=(shaped(2 * size, size), shaped(2...]
    ppermute x14, starting transfers between devices: 4.45 us -> 6.6 us  [swap(): lax.ppermute(block, axis, [(i, i ^ bit) for i in range(lax.axis_size(axis...]
    ppermute x4, waiting for transfers between devices: 24.6 us -> 22.6 us  [hop(): lax.ppermute(block, axis, [(i, (i + 2) % size) for i in range(parity, siz...]
  transfers between devices with their start and end apart: 24 -> 24, of which waited for: 17 -> 18; matrix products, arithmetic and copies ran while one was open for 0% -> 0% of each run, Pallas kernels for 19% -> 21%
where the time goes in v2:
time: 117 us
  waiting for transfers between devices  60.2 us (51%)
  Pallas kernels  30 us (26%)
  starting transfers between devices  25.4 us (22%)
    ppermute x14, waiting for transfers between devices, swap(): lax.ppermute(block, axis, [(i, i ^ bit) for i in range(lax.axis_size(axis...  29.4 us
    ppermute x4, waiting for transfers between devices, hop(): lax.ppermute(block, axis, [(i, (i + 2) % size) for i in range(parity, siz...  22.6 us
    ppermute x4, starting transfers between devices, hop(): lax.ppermute(block, axis, [(i, (i + 2) % size) for i in range(parity, siz...  10.4 us
    ppermute x6, starting transfers between devices, from_behind(): return lax.ppermute(block, axis, route)  8.36 us
    ppermute x6, waiting for transfers between devices, from_behind(): return lax.ppermute(block, axis, route)  8.15 us
    pallas_call x1, Pallas kernels, second_rounds(): pl.pallas_call(second_kernel, out_shape=(shaped(2 * size, size), shaped(2...  7.69 us
    ppermute x14, starting transfers between devices, swap(): lax.ppermute(block, axis, [(i, i ^ bit) for i in range(lax.axis_size(axis...  6.6 us
    pallas_call x1, Pallas kernels, first_rounds(): pl.pallas_call(first_kernel, out_shape=(shaped(2 * size, size), shaped(2...  6.56 us
  transfers between devices with their start and end apart: 24, of which 18 were waited for; matrix products, arithmetic and copies ran while one was open for 0% of the time, Pallas kernels for 21%

profile of v2, /device:TPU:26, one launch (start us, length us, event | category | flops | bytes accessed | tf_op | source)
XLA Modules:
  0.0 116.7 jit_solution(1450391905539140271)
XLA Ops:
  0.7 2.5 %early_rows.1 = f32[768,256]{1,0:T(8,128)} custom-call(f32[4096,256]{1,0:T(8,128)} %jac_ref.2, f32[32,128]{1,0:T(8,128)} %bitcast.3, f32[1,256]{1,0:T(1,128)} %bitcast.5), custom_call_target="tpu_custom_call" | custom-call | flops 1000 | bytes 1000 | tf_op jit(solution)/shard_map/early_rows/pallas_call | solution.py:147
  3.1 1.5 %collective-permute-start.3 = (f32[768,256]{1,0:T(8,128)}, f32[768,256]{1,0:T(8,128)S(1)}, u32[]{:S(2)}, u32[]{:S(2)}) collective-permute-start(f32[768,256]{1,0:T(8,128)} %early_rows.1), channel_id=1, source_target_pairs={{3,0},{0,1},{1,2},{2,3},{7,4},{4,5},{5,6},{6,7},{11,8},{8,9},{9,10... | collective-permute-start | bytes 2359304 | tf_op jit(solution)/shard_map/ppermute | solution.py:37
  4.7 3.4 %scaled_gram.1 = (f32[4096,256]{1,0:T(8,128)S(1)}, f32[192,128]{1,0:T(8,128)S(1)}, f32[192,128]{1,0:T(8,128)S(1)}) custom-call(f32[4096,256]{1,0:T(8,128)S(1)} %copy-done, f32[32,128]{1,0:T(8,128)S(1)} %bitcast.4, f32[1,256]{1,0:T(1,128)S(1)} %bitcast.6), custom_call_target="tpu_custom_call" | custom-call | flops 1000 | bytes 1000 | tf_op jit(solution)/shard_map/scaled_gram/pallas_call | solution.py:224
  8.2 1.5 %collective-permute-start.8 = (f32[1152,256]{1,0:T(8,128)S(1)}, f32[1152,256]{1,0:T(8,128)S(1)}, u32[]{:S(2)}, u32[]{:S(2)}) collective-permute-start(f32[1152,256]{1,0:T(8,128)S(1)} %rows_of.1), channel_id=1, source_target_pairs={{3,0},{0,1},{1,2},{2,3},{7,4},{4,5},{5,6},{6,7},{11,8},{8,9},{9,10... | collective-permute-start | bytes 3538952 | tf_op jit(solution)/shard_map/ppermute | solution.py:37
  9.7 1.3 %collective-permute-done = f32[192,128]{1,0:T(8,128)S(1)} collective-permute-done((f32[192,128]{1,0:T(8,128)S(1)}, f32[192,128]{1,0:T(8,128)S(1)}, u32[]{:S(2)}, u32[]{:S(2)}) %collective-permute-start) | collective-permute-done | bytes 98336 | tf_op jit(solution)/shard_map/ppermute | solution.py:41
  11.1 0.5 collective-permute-start.1
  11.6 4.4 %collective-permute-done.1 = f32[192,128]{1,0:T(8,128)S(1)} collective-permute-done((f32[192,128]{1,0:T(8,128)S(1)}, f32[192,128]{1,0:T(8,128)S(1)}, u32[]{:S(2)}, u32[]{:S(2)}) %collective-permute-start.1) | collective-permute-done | bytes 98336 | tf_op jit(solution)/shard_map/ppermute | solution.py:41
  16.0 0.4 collective-permute-start.2
  16.4 6.6 %collective-permute-done.2 = f32[192,128]{1,0:T(8,128)S(1)} collective-permute-done((f32[192,128]{1,0:T(8,128)S(1)}, f32[192,128]{1,0:T(8,128)S(1)}, u32[]{:S(2)}, u32[]{:S(2)}) %collective-permute-start.2) | collective-permute-done | bytes 98336 | tf_op jit(solution)/shard_map/ppermute | solution.py:41
  23.1 0.8 collective-permute-done.3.refs_2_
  23.8 0.5 collective-permute-done.4.other_ref
  24.4 6.6 %first_rounds.1 = (f32[256,128]{1,0:T(8,128)S(1)}, f32[256,128]{1,0:T(8,128)S(1)}, f32[160,128]{1,0:T(8,128)S(1)}, f32[128,128]{1,0:T(8,128)S(1)}, f32[128,128]{1,0:T(8,128)S(1)}, /*index=5*/f32[128,128]{1,0:T(8,128)S(1)}) custom-call(s32[2]{0:T(128)S(1)} %copy-done.3, s32[2]{0:T(128)S(1)} %bitcast.7, f32[192,128]{1,0:T(8,128)S(1)} %add.20.own_ref, ...), custom_call_target="tpu_custom_call" | custom-call | flops 1000 | bytes 1000 | tf_op jit(solution)/shard_map/first_rounds/pallas_call | solution.py:360
  30.9 0.4 travel_0.1.block_ref
  31.4 2.9 %collective-permute-start.5 = (f32[1152,128]{1,0:T(8,128)S(1)}, f32[1152,128]{1,0:T(8,128)S(1)}, u32[]{:S(2)}, u32[]{:S(2)}) collective-permute-start(f32[1152,128]{1,0:T(8,128)S(1)} %travel_0.1.block_ref), channel_id=1, source_target_pairs={{1,3},{3,1},{5,7},{7,5},{9,11},{11,9},{13,15},{15,13},{17,19},{19,... | collective-permute-start | bytes 1769480 | tf_op jit(solution)/shard_map/ppermute | solution.py:46
  34.4 0.5 travel_1.1.block_ref
  34.8 0.7 travel_early.1
  35.5 1.3 %stay_rows.1 = (f32[4224,128]{1,0:T(8,128)S(1)}, f32[1024,128]{1,0:T(8,128)S(1)}, f32[1280,128]{1,0:T(8,128)S(1)}) custom-call(f32[4096,256]{1,0:T(8,128)S(1)} %get-tuple-element.55.refs_0_.x_ref, f32[256,128]{1,0:T(8,128)S(1)} %get-tuple-element.62.turn_ref, f32[128,128]{1,0:T(8,128)S(1)} %get-tuple-element.63.head_ref), custom_call_target="tpu_custom_call" | custom-call | flops 1000 | bytes 1000 | tf_op jit(solution)/shard_map/stay_rows/pallas_call | solution.py:468
  36.8 11.8 %collective-permute-done.5.behind_ref.refs_5_ = f32[1152,128]{1,0:T(8,128)S(1)} collective-permute-done((f32[1152,128]{1,0:T(8,128)S(1)}, f32[1152,128]{1,0:T(8,128)S(1)}, u32[]{:S(2)}, u32[]{:S(2)}) %collective-permute-start.5) | collective-permute-done | bytes 589856 | tf_op jit(solution)/shard_map/ppermute | solution.py:46
  48.6 0.5 collective-permute-start.6
  49.2 0.5 collective-permute-done.7.first_ref
  49.7 1.5 %collective-permute-start.9 = (f32[1152,128]{1,0:T(8,128)S(1)}, f32[1152,128]{1,0:T(8,128)S(1)}, u32[]{:S(2)}, u32[]{:S(2)}) collective-permute-start(f32[1152,128]{1,0:T(8,128)S(1)} %pass_0.1), channel_id=1, source_target_pairs={{0,1},{1,0},{2,3},{3,2},{4,5},{5,4},{6,7},{7,6},{8,9},{9,8},{10,11... | collective-permute-start | bytes 1769480 | tf_op jit(solution)/shard_map/ppermute | solution.py:41
  51.3 0.4 collective-permute-start.10
  51.7 4.0 %collective-permute-done.10.second_ref = f32[160,128]{1,0:T(8,128)S(1)} collective-permute-done((f32[160,128]{1,0:T(8,128)S(1)}, f32[160,128]{1,0:T(8,128)S(1)}, u32[]{:S(2)}, u32[]{:S(2)}) %collective-permute-start.10) | collective-permute-done | bytes 81952 | tf_op jit(solution)/shard_map/ppermute | solution.py:41
  55.8 1.4 %collective-permute-done.11.refs_4_ = f32[320,128]{1,0:T(8,128)S(1)} collective-permute-done((f32[320,128]{1,0:T(8,128)S(1)}, f32[320,128]{1,0:T(8,128)S(1)}, u32[]{:S(2)}, u32[]{:S(2)}) %collective-permute-start.11) | collective-permute-done | bytes 163872 | tf_op jit(solution)/shard_map/ppermute | solution.py:41
  57.2 1.5 %near_rows.1 = (f32[1920,128]{1,0:T(8,128)S(1)}, f32[1920,128]{1,0:T(8,128)S(1)}, f32[128,128]{1,0:T(8,128)S(1)}, f32[128,128]{1,0:T(8,128)S(1)}) custom-call(f32[4224,128]{1,0:T(8,128)S(1)} %get-tuple-element.66.refs_0_.stay_ref, f32[1152,256]{1,0:T(8,128)S(1)} %collective-permute-done.8.refs_1_, f32[768,256]{1,0:T(8,128)S(1)} %collective-permute-done.3.refs_2_, ...), custom_call_target="tpu_custom_call" | custom-call | flops 1000 | bytes 1000 | tf_op jit(solution)/shard_map/near_rows/pallas_call | solution.py:537
  58.7 3.4 %collective-permute-start.12 = (f32[1024,128]{1,0:T(8,128)S(1)}, f32[1024,128]{1,0:T(8,128)S(1)}, u32[]{:S(2)}, u32[]{:S(2)}) collective-permute-start(f32[1024,128]{1,0:T(8,128)S(1)} %get-tuple-element.76.block_ref), channel_id=1, source_target_pairs={{1,3},{3,1},{5,7},{7,5},{9,11},{11,9},{13,15},{15,13},{17,19},{19,... | collective-permute-start | bytes 1572872 | tf_op jit(solution)/shard_map/ppermute | solution.py:46
  62.1 1.1 collective-permute-done.6.behind_ref.refs_7_
  63.3 0.7 collective-permute-done.9.arrived_ref.refs_1_
  63.9 1.5 %collective-permute-start.13 = (f32[1152,128]{1,0:T(8,128)S(1)}, f32[1152,128]{1,0:T(8,128)S(1)}, u32[]{:S(2)}, u32[]{:S(2)}) collective-permute-start(f32[1152,128]{1,0:T(8,128)S(1)} %pass_1.1), channel_id=1, source_target_pairs={{0,1},{1,0},{2,3},{3,2},{4,5},{5,4},{6,7},{7,6},{8,9},{9,8},{10,11... | collective-permute-start | bytes 1769480 | tf_op jit(solution)/shard_map/ppermute | solution.py:41
  65.4 0.7 collective-permute-start.15
  66.1 8.5 %collective-permute-done.12.behind_ref = f32[1024,128]{1,0:T(8,128)S(1)} collective-permute-done((f32[1024,128]{1,0:T(8,128)S(1)}, f32[1024,128]{1,0:T(8,128)S(1)}, u32[]{:S(2)}, u32[]{:S(2)}) %collective-permute-start.12) | collective-permute-done | bytes 524320 | tf_op jit(solution)/shard_map/ppermute | solution.py:46
  74.6 3.4 %collective-permute-start.14 = (f32[1280,128]{1,0:T(8,128)S(1)}, f32[1280,128]{1,0:T(8,128)S(1)}, u32[]{:S(2)}, u32[]{:S(2)}) collective-permute-start(f32[1280,128]{1,0:T(8,128)S(1)} %get-tuple-element.99.block_ref), channel_id=1, source_target_pairs={{1,3},{3,1},{5,7},{7,5},{9,11},{11,9},{13,15},{15,13},{17,19},{19,... | collective-permute-start | bytes 1966088 | tf_op jit(solution)/shard_map/ppermute | solution.py:46
  78.1 1.1 collective-permute-start.19
  79.2 0.4 add_cross.1.before_ref
  79.6 0.4 last_cross.1
  80.0 1.6 %collective-permute-start.21 = (f32[1920,128]{1,0:T(8,128)S(1)}, f32[1920,128]{1,0:T(8,128)S(1)}, u32[]{:S(2)}, u32[]{:S(2)}) collective-permute-start(f32[1920,128]{1,0:T(8,128)S(1)} %travel_early.1), channel_id=1, source_target_pairs={{2,0},{3,1},{0,2},{1,3},{6,4},{7,5},{4,6},{5,7},{10,8},{11,9},{8,1... | collective-permute-start | bytes 2949128 | tf_op jit(solution)/shard_map/ppermute | solution.py:37
  81.6 1.2 %collective-permute-done.16 = f32[64,128]{1,0:T(8,128)S(1)} collective-permute-done((f32[64,128]{1,0:T(8,128)S(1)}, f32[64,128]{1,0:T(8,128)S(1)}, u32[]{:S(2)}, u32[]{:S(2)}) %collective-permute-start.16) | collective-permute-done | bytes 32800 | tf_op jit(solution)/shard_map/ppermute | solution.py:41
  82.8 0.5 collective-permute-start.17
  83.3 3.5 %collective-permute-done.17 = f32[64,128]{1,0:T(8,128)S(1)} collective-permute-done((f32[64,128]{1,0:T(8,128)S(1)}, f32[64,128]{1,0:T(8,128)S(1)}, u32[]{:S(2)}, u32[]{:S(2)}) %collective-permute-start.17) | collective-permute-done | bytes 32800 | tf_op jit(solution)/shard_map/ppermute | solution.py:41
  86.8 0.3 collective-permute-start.18
  87.1 4.7 %collective-permute-done.18 = f32[64,128]{1,0:T(8,128)S(1)} collective-permute-done((f32[64,128]{1,0:T(8,128)S(1)}, f32[64,128]{1,0:T(8,128)S(1)}, u32[]{:S(2)}, u32[]{:S(2)}) %collective-permute-start.18) | collective-permute-done | bytes 32800 | tf_op jit(solution)/shard_map/ppermute | solution.py:41
  91.8 2.3 %collective-permute-done.14.behind_ref = f32[1280,128]{1,0:T(8,128)S(1)} collective-permute-done((f32[1280,128]{1,0:T(8,128)S(1)}, f32[1280,128]{1,0:T(8,128)S(1)}, u32[]{:S(2)}, u32[]{:S(2)}) %collective-permute-start.14) | collective-permute-done | bytes 655392 | tf_op jit(solution)/shard_map/ppermute | solution.py:46
  94.3 1.2 %collective-permute-done.20.other_ref = f32[64,128]{1,0:T(8,128)S(1)} collective-permute-done((f32[64,128]{1,0:T(8,128)S(1)}, f32[64,128]{1,0:T(8,128)S(1)}, u32[]{:S(2)}, u32[]{:S(2)}) %collective-permute-start.20) | collective-permute-done | bytes 32800 | tf_op jit(solution)/shard_map/ppermute | solution.py:41
  95.5 7.7 %second_rounds.1 = (f32[256,128]{1,0:T(8,128)S(1)}, f32[256,128]{1,0:T(8,128)S(1)}) custom-call(s32[2]{0:T(128)S(1)} %copy-done.3, s32[2]{0:T(128)S(1)} %bitcast.8, f32[64,128]{1,0:T(8,128)S(1)} %add.23.own_ref, f32[64,128]{1,0:T(8,128)S(1)} %collective-permute-done.20.other_ref, f32[128,128]{1,0:T(8,128)S(1)} %get-tuple-element.92.gram_ref, ...), custom_call_target="tpu_custom_call" | custom-call | flops 1000 | bytes 1000 | tf_op jit(solution)/shard_map/second_rounds/pallas_call | solution.py:406
  103.2 3.1 %collective-permute-start.22 = (f32[256,128]{1,0:T(8,128)S(1)}, f32[256,128]{1,0:T(8,128)S(1)}, u32[]{:S(2)}, u32[]{:S(2)}) collective-permute-start(f32[256,128]{1,0:T(8,128)S(1)} %get-tuple-element.97), channel_id=1, source_target_pairs={{3,0},{0,1},{1,2},{2,3},{7,4},{4,5},{5,6},{6,7},{11,8},{8,9},{9,10... | collective-permute-start | bytes 393224 | tf_op jit(solution)/shard_map/ppermute | solution.py:37
  106.4 1.3 %staying.1.refs_0_ = f32[4224,128]{1,0:T(8,128)S(1)} custom-call(f32[4224,128]{1,0:T(8,128)S(1)} %get-tuple-element.66.refs_0_.stay_ref, f32[1152,128]{1,0:T(8,128)S(1)} %collective-permute-done.9.arrived_ref.refs_1_, f32[1152,128]{1,0:T(8,128)S(1)} %collective-permute-done.13.arrived_ref.refs_2_, f32[1920,128]{1,0:T(8,128)S(1)} %get-tuple-element.79.refs_3_, ...), custom_call_target="tpu_custom_call" | custom-call | flops 1000 | bytes 1000 | tf_op jit(solution)/shard_map/staying/pallas_call | solution.py:600
  107.7 5.8 %collective-permute-done.21.refs_8_ = f32[1920,128]{1,0:T(8,128)S(1)} collective-permute-done((f32[1920,128]{1,0:T(8,128)S(1)}, f32[1920,128]{1,0:T(8,128)S(1)}, u32[]{:S(2)}, u32[]{:S(2)}) %collective-permute-start.21) | collective-permute-done | bytes 983072 | tf_op jit(solution)/shard_map/ppermute | solution.py:37
  113.5 3.1 %arriving.1 = (f32[4096,256]{1,0:T(8,128)}, f32[128,256]{1,0:T(8,128)}) custom-call(f32[4224,128]{1,0:T(8,128)S(1)} %staying.1.refs_0_, f32[256,128]{1,0:T(8,128)S(1)} %collective-permute-done.22.refs_1_, f32[1024,128]{1,0:T(8,128)S(1)} %collective-permute-done.19.refs_2_, f32[1280,128]{1,0:T(8,128)S(1)} %collective-permute-done.23.refs_3_, ...), custom_call_target="tpu_custom_call" | custom-call | flops 1000 | bytes 1000 | tf_op jit(solution)/shard_map/arriving/pallas_call | solution.py:678
  (35 shorter events, 0.7 us)
Async XLA Ops:
  0.6 4.1 %copy-start = (f32[4096,256]{1,0:T(8,128)S(1)}, f32[4096,256]{1,0:T(8,128)}, u32[]{:S(2)}) copy-start(f32[4096,256]{1,0:T(8,128)} %jac_ref.2) | copy-start | bytes 12582916
  0.6 4.1 %copy-start.1 = (f32[4096]{0:T(1024)S(1)}, f32[4096]{0:T(1024)}, u32[]{:S(2)}) copy-start(f32[4096]{0:T(1024)} %param.6) | copy-start | bytes 49156
  0.6 4.0 %copy-start.2 = (f32[256]{0:T(256)S(1)}, f32[256]{0:T(256)}, u32[]{:S(2)}) copy-start(f32[256]{0:T(256)} %param.7) | copy-start | bytes 3076
  3.1 20.7 %collective-permute-start.3 = (f32[768,256]{1,0:T(8,128)}, f32[768,256]{1,0:T(8,128)S(1)}, u32[]{:S(2)}, u32[]{:S(2)}) collective-permute-start(f32[768,256]{1,0:T(8,128)} %early_rows.1), channel_id=1, source_target_pairs={{3,0},{0,1},{1,2},{2,3},{7,4},{4,5},{5,6},{6,7},{11,8},{8,9},{9,10... | collective-permute-start | bytes 2359304 | tf_op jit(solution)/shard_map/ppermute | solution.py:37
  8.1 16.3 %copy-start.3 = (s32[2]{0:T(128)S(1)}, s32[2]{0:T(128)}, u32[]{:S(2)}) copy-start(s32[2]{0:T(128)} %count_ref.3) | copy-start | bytes 28
  8.1 16.3 %copy-start.4 = (s32[2,1]{0,1:T(1,128)S(1)}, s32[2,1]{0,1:T(1,128)}, u32[]{:S(2)}) copy-start(s32[2,1]{0,1:T(1,128)} %param.9) | copy-start | bytes 28
  8.2 41.5 %collective-permute-start.8 = (f32[1152,256]{1,0:T(8,128)S(1)}, f32[1152,256]{1,0:T(8,128)S(1)}, u32[]{:S(2)}, u32[]{:S(2)}) collective-permute-start(f32[1152,256]{1,0:T(8,128)S(1)} %rows_of.1), channel_id=1, source_target_pairs={{3,0},{0,1},{1,2},{2,3},{7,4},{4,5},{5,6},{6,7},{11,8},{8,9},{9,10... | collective-permute-start | bytes 3538952 | tf_op jit(solution)/shard_map/ppermute | solution.py:37
  9.7 1.3 %collective-permute-start = (f32[192,128]{1,0:T(8,128)S(1)}, f32[192,128]{1,0:T(8,128)S(1)}, u32[]{:S(2)}, u32[]{:S(2)}) collective-permute-start(f32[192,128]{1,0:T(8,128)S(1)} %get-tuple-element.57), channel_id=1, source_target_pairs={{0,4},{4,0},{8,12},{12,8},{16,20},{20,16},{24,28},{28,24},{1,5},{5... | collective-permute-start | bytes 294920 | tf_op jit(solution)/shard_map/ppermute | solution.py:41
  11.1 4.9 %collective-permute-start.1 = (f32[192,128]{1,0:T(8,128)S(1)}, f32[192,128]{1,0:T(8,128)S(1)}, u32[]{:S(2)}, u32[]{:S(2)}) collective-permute-start(f32[192,128]{1,0:T(8,128)S(1)} %add.18), channel_id=1, source_target_pairs={{0,8},{4,12},{8,0},{12,4},{16,24},{20,28},{24,16},{28,20},{1,9},{5... | collective-permute-start | bytes 294920 | tf_op jit(solution)/shard_map/ppermute | solution.py:41
  16.0 7.0 %collective-permute-start.2 = (f32[192,128]{1,0:T(8,128)S(1)}, f32[192,128]{1,0:T(8,128)S(1)}, u32[]{:S(2)}, u32[]{:S(2)}) collective-permute-start(f32[192,128]{1,0:T(8,128)S(1)} %add.19), channel_id=1, source_target_pairs={{0,16},{4,20},{8,24},{12,28},{16,0},{20,4},{24,8},{28,12},{1,17},{... | collective-permute-start | bytes 294920 | tf_op jit(solution)/shard_map/ppermute | solution.py:41
  23.0 1.4 %collective-permute-start.4 = (f32[192,128]{1,0:T(8,128)S(1)}, f32[192,128]{1,0:T(8,128)S(1)}, u32[]{:S(2)}, u32[]{:S(2)}) collective-permute-start(f32[192,128]{1,0:T(8,128)S(1)} %add.20.own_ref), channel_id=1, source_target_pairs={{0,4},{4,0},{8,12},{12,8},{16,20},{20,16},{24,28},{28,24},{1,5},{5... | collective-permute-start | bytes 294920 | tf_op jit(solution)/shard_map/ppermute | solution.py:41
  31.4 17.3 %collective-permute-start.5 = (f32[1152,128]{1,0:T(8,128)S(1)}, f32[1152,128]{1,0:T(8,128)S(1)}, u32[]{:S(2)}, u32[]{:S(2)}) collective-permute-start(f32[1152,128]{1,0:T(8,128)S(1)} %travel_0.1.block_ref), channel_id=1, source_target_pairs={{1,3},{3,1},{5,7},{7,5},{9,11},{11,9},{13,15},{15,13},{17,19},{19,... | collective-permute-start | bytes 1769480 | tf_op jit(solution)/shard_map/ppermute | solution.py:46
  34.3 15.4 %collective-permute-start.7 = (f32[160,128]{1,0:T(8,128)S(1)}, f32[160,128]{1,0:T(8,128)S(1)}, u32[]{:S(2)}, u32[]{:S(2)}) collective-permute-start(f32[160,128]{1,0:T(8,128)S(1)} %get-tuple-element.68), channel_id=1, source_target_pairs={{3,0},{0,1},{1,2},{2,3},{7,4},{4,5},{5,6},{6,7},{11,8},{8,9},{9,10... | collective-permute-start | bytes 245768 | tf_op jit(solution)/shard_map/ppermute | solution.py:37
  48.6 14.6 %collective-permute-start.6 = (f32[1152,128]{1,0:T(8,128)S(1)}, f32[1152,128]{1,0:T(8,128)S(1)}, u32[]{:S(2)}, u32[]{:S(2)}) collective-permute-start(f32[1152,128]{1,0:T(8,128)S(1)} %travel_1.1.block_ref), channel_id=1, source_target_pairs={{2,0},{3,1},{0,2},{1,3},{6,4},{7,5},{4,6},{5,7},{10,8},{11,9},{8,1... | collective-permute-start | bytes 1769480 | tf_op jit(solution)/shard_map/ppermute | solution.py:37
  49.7 14.2 %collective-permute-start.9 = (f32[1152,128]{1,0:T(8,128)S(1)}, f32[1152,128]{1,0:T(8,128)S(1)}, u32[]{:S(2)}, u32[]{:S(2)}) collective-permute-start(f32[1152,128]{1,0:T(8,128)S(1)} %pass_0.1), channel_id=1, source_target_pairs={{0,1},{1,0},{2,3},{3,2},{4,5},{5,4},{6,7},{7,6},{8,9},{9,8},{10,11... | collective-permute-start | bytes 1769480 | tf_op jit(solution)/shard_map/ppermute | solution.py:41
  51.3 4.4 %collective-permute-start.10 = (f32[160,128]{1,0:T(8,128)S(1)}, f32[160,128]{1,0:T(8,128)S(1)}, u32[]{:S(2)}, u32[]{:S(2)}) collective-permute-start(f32[160,128]{1,0:T(8,128)S(1)} %collective-permute-done.7.first_ref), channel_id=1, source_target_pairs={{0,8},{4,12},{8,0},{12,4},{16,24},{20,28},{24,16},{28,20},{1,9},{5... | collective-permute-start | bytes 245768 | tf_op jit(solution)/shard_map/ppermute | solution.py:41
  55.7 1.5 %collective-permute-start.11 = (f32[320,128]{1,0:T(8,128)S(1)}, f32[320,128]{1,0:T(8,128)S(1)}, u32[]{:S(2)}, u32[]{:S(2)}) collective-permute-start(f32[320,128]{1,0:T(8,128)S(1)} %joined.1.refs_3_), channel_id=1, source_target_pairs={{0,4},{4,0},{8,12},{12,8},{16,20},{20,16},{24,28},{28,24},{1,5},{5... | collective-permute-start | bytes 491528 | tf_op jit(solution)/shard_map/ppermute | solution.py:41
  58.7 15.9 %collective-permute-start.12 = (f32[1024,128]{1,0:T(8,128)S(1)}, f32[1024,128]{1,0:T(8,128)S(1)}, u32[]{:S(2)}, u32[]{:S(2)}) collective-permute-start(f32[1024,128]{1,0:T(8,128)S(1)} %get-tuple-element.76.block_ref), channel_id=1, source_target_pairs={{1,3},{3,1},{5,7},{7,5},{9,11},{11,9},{13,15},{15,13},{17,19},{19,... | collective-permute-start | bytes 1572872 | tf_op jit(solution)/shard_map/ppermute | solution.py:46
  63.9 14.1 %collective-permute-start.13 = (f32[1152,128]{1,0:T(8,128)S(1)}, f32[1152,128]{1,0:T(8,128)S(1)}, u32[]{:S(2)}, u32[]{:S(2)}) collective-permute-start(f32[1152,128]{1,0:T(8,128)S(1)} %pass_1.1), channel_id=1, source_target_pairs={{0,1},{1,0},{2,3},{3,2},{4,5},{5,4},{6,7},{7,6},{8,9},{9,8},{10,11... | collective-permute-start | bytes 1769480 | tf_op jit(solution)/shard_map/ppermute | solution.py:41
  65.4 14.6 %collective-permute-start.15 = (f32[1152,128]{1,0:T(8,128)S(1)}, f32[1152,128]{1,0:T(8,128)S(1)}, u32[]{:S(2)}, u32[]{:S(2)}) collective-permute-start(f32[1152,128]{1,0:T(8,128)S(1)} %travel_0.1.block_ref), channel_id=1, source_target_pairs={{0,2},{2,0},{4,6},{6,4},{8,10},{10,8},{12,14},{14,12},{16,18},{18,... | collective-permute-start | bytes 1769480 | tf_op jit(solution)/shard_map/ppermute | solution.py:46
  74.6 19.6 %collective-permute-start.14 = (f32[1280,128]{1,0:T(8,128)S(1)}, f32[1280,128]{1,0:T(8,128)S(1)}, u32[]{:S(2)}, u32[]{:S(2)}) collective-permute-start(f32[1280,128]{1,0:T(8,128)S(1)} %get-tuple-element.99.block_ref), channel_id=1, source_target_pairs={{1,3},{3,1},{5,7},{7,5},{9,11},{11,9},{13,15},{15,13},{17,19},{19,... | collective-permute-start | bytes 1966088 | tf_op jit(solution)/shard_map/ppermute | solution.py:46
  78.1 13.8 %collective-permute-start.19 = (f32[1024,128]{1,0:T(8,128)S(1)}, f32[1024,128]{1,0:T(8,128)S(1)}, u32[]{:S(2)}, u32[]{:S(2)}) collective-permute-start(f32[1024,128]{1,0:T(8,128)S(1)} %pass_2.1), channel_id=1, source_target_pairs={{0,1},{1,0},{2,3},{3,2},{4,5},{5,4},{6,7},{7,6},{8,9},{9,8},{10,11... | collective-permute-start | bytes 1572872 | tf_op jit(solution)/shard_map/ppermute | solution.py:41
  80.0 33.4 %collective-permute-start.21 = (f32[1920,128]{1,0:T(8,128)S(1)}, f32[1920,128]{1,0:T(8,128)S(1)}, u32[]{:S(2)}, u32[]{:S(2)}) collective-permute-start(f32[1920,128]{1,0:T(8,128)S(1)} %travel_early.1), channel_id=1, source_target_pairs={{2,0},{3,1},{0,2},{1,3},{6,4},{7,5},{4,6},{5,7},{10,8},{11,9},{8,1... | collective-permute-start | bytes 2949128 | tf_op jit(solution)/shard_map/ppermute | solution.py:37
  81.6 1.2 %collective-permute-start.16 = (f32[64,128]{1,0:T(8,128)S(1)}, f32[64,128]{1,0:T(8,128)S(1)}, u32[]{:S(2)}, u32[]{:S(2)}) collective-permute-start(f32[64,128]{1,0:T(8,128)S(1)} %get-tuple-element.88), channel_id=1, source_target_pairs={{0,4},{4,0},{8,12},{12,8},{16,20},{20,16},{24,28},{28,24},{1,5},{5... | collective-permute-start | bytes 98312 | tf_op jit(solution)/shard_map/ppermute | solution.py:41
  82.8 3.9 %collective-permute-start.17 = (f32[64,128]{1,0:T(8,128)S(1)}, f32[64,128]{1,0:T(8,128)S(1)}, u32[]{:S(2)}, u32[]{:S(2)}) collective-permute-start(f32[64,128]{1,0:T(8,128)S(1)} %add.21), channel_id=1, source_target_pairs={{0,8},{4,12},{8,0},{12,4},{16,24},{20,28},{24,16},{28,20},{1,9},{5... | collective-permute-start | bytes 98312 | tf_op jit(solution)/shard_map/ppermute | solution.py:41
  86.8 5.1 %collective-permute-start.18 = (f32[64,128]{1,0:T(8,128)S(1)}, f32[64,128]{1,0:T(8,128)S(1)}, u32[]{:S(2)}, u32[]{:S(2)}) collective-permute-start(f32[64,128]{1,0:T(8,128)S(1)} %add.22), channel_id=1, source_target_pairs={{0,16},{4,20},{8,24},{12,28},{16,0},{20,4},{24,8},{28,12},{1,17},{... | collective-permute-start | bytes 98312 | tf_op jit(solution)/shard_map/ppermute | solution.py:41
  94.2 19.3 %collective-permute-start.23 = (f32[1280,128]{1,0:T(8,128)S(1)}, f32[1280,128]{1,0:T(8,128)S(1)}, u32[]{:S(2)}, u32[]{:S(2)}) collective-permute-start(f32[1280,128]{1,0:T(8,128)S(1)} %pass_3.1), channel_id=1, source_target_pairs={{0,1},{1,0},{2,3},{3,2},{4,5},{5,4},{6,7},{7,6},{8,9},{9,8},{10,11... | collective-permute-start | bytes 1966088 | tf_op jit(solution)/shard_map/ppermute | solution.py:41
  94.2 1.3 %collective-permute-start.20 = (f32[64,128]{1,0:T(8,128)S(1)}, f32[64,128]{1,0:T(8,128)S(1)}, u32[]{:S(2)}, u32[]{:S(2)}) collective-permute-start(f32[64,128]{1,0:T(8,128)S(1)} %add.23.own_ref), channel_id=1, source_target_pairs={{0,4},{4,0},{8,12},{12,8},{16,20},{20,16},{24,28},{28,24},{1,5},{5... | collective-permute-start | bytes 98312 | tf_op jit(solution)/shard_map/ppermute | solution.py:41
  103.2 10.2 %collective-permute-start.22 = (f32[256,128]{1,0:T(8,128)S(1)}, f32[256,128]{1,0:T(8,128)S(1)}, u32[]{:S(2)}, u32[]{:S(2)}) collective-permute-start(f32[256,128]{1,0:T(8,128)S(1)} %get-tuple-element.97), channel_id=1, source_target_pairs={{3,0},{0,1},{1,2},{2,3},{7,4},{4,5},{5,6},{6,7},{11,8},{8,9},{9,10... | collective-permute-start | bytes 393224 | tf_op jit(solution)/shard_map/ppermute | solution.py:37
